TPU v7x, 32 devices: a whole 2x2x4 slice. The times are simulated.
32 devices in a mesh: outer: 8 (over z, x), inner: 4 (over y, core).
Axes of the slice: x: 2, y: 2, z: 4, core: 2. Of those that a mesh axis runs over, the one named last changes fastest.
Arguments:
- queries: bfloat16 [8192, 1024], P(('outer', 'inner')), may hold values from -48 to 48
- keys: bfloat16 [8192, 128], P(('outer', 'inner')), may hold values from -4 to 4
- values: bfloat16 [8192, 128], P(('outer', 'inner')), may hold values from -6 to 6
- reflect: bfloat16 [8192, 128], P(('outer', 'inner')), may hold values from -6 to 6
- reflect_logit: float32 [8192], P(('outer', 'inner')), may hold values from -8 to 8
- doc_of_block: int32 [32], replicated, may hold values from 0 to 15, never falling along the last dimension, each value on 1 to 4 neighbouring positions
Outputs:
- attended: bfloat16 [8192, 1024], P(('outer', 'inner'))
Inputs may be any that keep to these rules, and one draw needn't show every extreme that they name: `doc_of_block`: document numbers never fall along the blocks; every document covers 1 to 4 consecutive blocks, and one covers exactly 4.
All inputs are finite; a program needn't handle non-finite values.
Results may differ from a plain program's by a relative error of at most 0.017.
Values may be sent and summed in bfloat16 or wider, within the bound.
No kernel may reach another device: no remote copies, remote signals or barrier semaphores. Data moves between devices by JAX's collectives and lax.ppermute only.
A program may use at most 64 MiB of HBM per device.

v0:
```python
import jax
import jax.numpy as jnp
from jax import lax
from jax.sharding import PartitionSpec as P


def passed_along(value, axis, steps):
    count = lax.axis_size(axis)
    initial, last = (max(0, -steps), min(count, count - steps))
    return lax.ppermute(value, axis, [(source, source + steps) for source in range(initial, last)])


def matmul(left_side, right_side):
    return jnp.dot(
        left_side, right_side, precision=lax.Precision.HIGHEST, preferred_element_type=jnp.float32
    )


def apply_map(vectors, matrix):
    return lax.dot_general(
        vectors,
        matrix,
        (((1,), (1,)), ((), ())),
        precision=lax.Precision.HIGHEST,
        preferred_element_type=jnp.float32,
    )


def unit_inverse(strict_part):
    length = strict_part.shape[0]
    identity = jnp.eye(length, dtype=jnp.float32)
    result = identity - strict_part
    power = strict_part
    reach = 2
    while reach < length:
        power = matmul(power, power)
        result = matmul(result, identity + power)
        reach = reach * 2
    return result


def prepare(queries, keys, reflect, reflect_logit):
    length = keys.shape[0]
    head_size = keys.shape[1]
    head_count = queries.shape[1] // head_size
    direction = reflect.astype(jnp.float32)
    direction = direction * lax.rsqrt(jnp.sum(direction * direction, axis=1, keepdims=True) + 1e-06)
    strength = 2.0 * jax.nn.sigmoid(reflect_logit)
    scaled_dirs = direction * strength[:, None]
    places = jnp.arange(length)
    strictly = places[:, None] > places[None, :]
    intersection = apply_map(direction, direction)
    lower_inverse = unit_inverse(jnp.where(strictly, intersection, 0.0) * strength[None, :])
    upper_inverse = unit_inverse(jnp.where(strictly.T, intersection, 0.0) * strength[None, :])
    key_float = keys.astype(jnp.float32)
    updates = matmul(lower_inverse, jnp.where(strictly, apply_map(direction, key_float), 0.0))
    key_end = key_float - matmul(updates.T, scaled_dirs)
    reflected = matmul(lower_inverse, direction)
    transit = jnp.eye(head_size, dtype=jnp.float32) - matmul(scaled_dirs.T, reflected)
    query_rows = (
        queries.reshape(length, head_count, head_size)
        .transpose(1, 0, 2)
        .reshape(head_count * length, head_size)
    )
    query_float = query_rows.astype(jnp.float32)
    facing = apply_map(query_float, direction)
    query_places = jnp.tile(places, head_count)
    visible = places[None, :] <= query_places[:, None]
    solved = matmul(upper_inverse, jnp.where(visible.T, facing.T, 0.0))
    query_turned = (query_float - matmul(solved.T, scaled_dirs)).astype(jnp.bfloat16)
    direct = lax.dot_general(
        query_rows, keys, (((1,), (1,)), ((), ())), preferred_element_type=jnp.float32
    )
    inside = (
        direct - matmul(jnp.where(visible, facing, 0.0) * strength[None, :], updates)
    ) * head_size ** (-0.5)
    inside = jnp.where(visible, inside, -1e30)
    return (query_turned, inside, key_end, transit)


def opening_state(inside, values):
    row_peak = jnp.max(inside, axis=1, keepdims=True)
    powers = jnp.exp(inside - row_peak)
    weight_sum = jnp.sum(powers, axis=1, keepdims=True)
    weighted = jnp.dot(powers.astype(jnp.bfloat16), values, preferred_element_type=jnp.float32)
    return (row_peak, weight_sum, weighted)


def absorb(softmax_state, query_turned, key_block, value_block, score_scale):
    old_peak, weight_sum, weighted = softmax_state
    scores = (
        lax.dot_general(
            query_turned,
            key_block.astype(jnp.bfloat16),
            (((1,), (1,)), ((), ())),
            preferred_element_type=jnp.float32,
        )
        * score_scale
    )
    new_peak = jnp.maximum(old_peak, jnp.max(scores, axis=1, keepdims=True))
    powers = jnp.exp(scores - new_peak)
    factor = jnp.exp(old_peak - new_peak)
    weight_sum = weight_sum * factor + jnp.sum(powers, axis=1, keepdims=True)
    weighted = weighted * factor + jnp.dot(
        powers.astype(jnp.bfloat16), value_block, preferred_element_type=jnp.float32
    )
    return (new_peak, weight_sum, weighted)


def local(queries, keys, values, reflect, reflect_logit, doc_of_block):
    inner_count = lax.axis_size("inner")
    outer_count = lax.axis_size("outer")
    longest = inner_count * outer_count // 8
    last_block = inner_count * outer_count - 1
    inner_pos = lax.axis_index("inner")
    outer_pos = lax.axis_index("outer")
    block_pos = outer_pos * inner_count + inner_pos
    own_doc = doc_of_block[block_pos]
    head_size = keys.shape[1]
    head_count = queries.shape[1] // head_size
    length = keys.shape[0]
    score_scale = head_size ** (-0.5)
    query_turned, inside, key_end, transit = prepare(queries, keys, reflect, reflect_logit)
    softmax_state = opening_state(inside, values)

    def visit(current, source, key_block, value_block):
        wanted = (source >= 0) & (doc_of_block[jnp.clip(source, 0, last_block)] == own_doc)

        def include(present):
            return absorb(present, query_turned, key_block, value_block, score_scale)

        return lax.cond(wanted, include, lambda present: present, current)

    def chain_step(travel, carry_state):
        current, moving_keys, moving_values = carry_state
        got_keys = passed_along(moving_keys.astype(jnp.bfloat16), ("outer", "inner"), 1).astype(
            moving_keys.dtype
        )
        got_values = passed_along(moving_values, ("outer", "inner"), 1)
        current = visit(current, block_pos - travel, got_keys, got_values)
        return (current, apply_map(got_keys, transit), got_values)

    softmax_state, spent_keys, spent_values = lax.fori_loop(
        1, longest, chain_step, (softmax_state, key_end, values)
    )
    row_peak, weight_sum, weighted = softmax_state
    result = (weighted / weight_sum).reshape(head_count, length, head_size).transpose(1, 0, 2)
    return result.reshape(length, head_count * head_size).astype(jnp.bfloat16)


def solution(mesh):
    placed = (
        P(("outer", "inner"), None),
        P(("outer", "inner"), None),
        P(("outer", "inner"), None),
        P(("outer", "inner"), None),
        P(("outer", "inner")),
        P(),
    )
    return jax.shard_map(
        local, mesh=mesh, in_specs=placed, out_specs=P(("outer", "inner"), None), check_vma=False
    )
```

profile of v0, /device:TPU:8, one launch (start us, length us, event | category | flops | bytes accessed | tf_op | source)
XLA Modules:
  0.0 61.8 jit_solution(3731461730045425780)
XLA Ops:
  0.0 0.9 %copy.40 = bf16[256,128]{1,0:T(8,128)(2,1)S(1)} copy(bf16[256,128]{1,0:T(8,128)(2,1)} %param.12) | data formatting | bytes 131072
  0.9 1.2 %dynamic_slice.10 = s32[1]{0:T(128)} dynamic-slice(s32[32]{0:T(128)} %param.15, s32[]{:T(128)S(6)} %select_n.31), dynamic_slice_sizes={1} | dynamic-slice | bytes 12 | tf_op jit(solution)/shard_map/dynamic_slice | solution.py:118
  2.1 0.9 %fusion.43 = f32[256]{0:T(256)S(1)} fusion(bf16[256,128]{1,0:T(8,128)(2,1)} %param.13), kind=kLoop, calls=%fused_computation.77 | loop fusion | flops 98048 | bytes 66560 | tf_op jit(solution)/shard_map/reduce_sum | solution.py:47
  3.1 0.7 %divide_multiply_fusion = (f32[256]{0:T(256)S(1)}, f32[256]{0:T(256)S(1)}) fusion(f32[256]{0:T(256)} %param.14, f32[256]{0:T(256)S(1)} %fusion.43), kind=kLoop, calls=%fused_computation.98 | loop fusion | flops 1280 | bytes 4096 | tf_op jit(solution)/shard_map/mul | solution.py:48
  3.8 1.4 %fusion.38 = f32[256,256]{1,0:T(8,128)S(1)} fusion(bf16[256,128]{1,0:T(8,128)(2,1)} %param.13, f32[256]{0:T(256)S(1)} %get-tuple-element.254), kind=kOutput, calls=%fused_computation.75 | convolution fusion | flops 100728832 | bytes 328704 | tf_op jit(solution)/shard_map/dot_general | solution.py:20
  16.3 0.5 fusion.36
  16.8 0.5 convolution_subtract_fusion.3
  18.0 0.9 %convolution_subtract_fusion.2 = bf16[256,128]{1,0:T(8,128)(2,1)S(1)} fusion(f32[256,256]{1,0:T(8,128)S(1)} %fusion.78, bf16[256,128]{1,0:T(8,128)(2,1)S(1)} %copy-done.1, bf16[256,128]{1,0:T(8,128)(2,1)S(1)} %copy-done.2, f32[256]{0:T(256)S(1)} %get-tuple-element.253, f32[256]{0:T(256)S(1)} %get-tuple-element.254), kind=kOutput, calls=%fused_computation.40 | convolution fusion | flops 100859904 | bytes 460800 | tf_op jit(solution)/shard_map/dot_general | solution.py:14
  19.0 1.0 %fusion.39 = f32[256,2048]{1,0:T(8,128)S(1)} fusion(bf16[2048,128]{1,0:T(8,128)(2,1)S(1)} %bitcast.95, bf16[256,128]{1,0:T(8,128)(2,1)S(1)} %copy-done.1, f32[256]{0:T(256)S(1)} %get-tuple-element.254), kind=kOutput, calls=%fused_computation.76 | convolution fusion | flops 805371904 | bytes 2688000 | tf_op jit(solution)/shard_map/dot_general | solution.py:20
  20.0 2.0 %fusion.10 = f32[256,2048]{1,0:T(8,128)S(1)} fusion(f32[256,256]{1,0:T(8,128)S(1)} %fusion.84, f32[256,2048]{1,0:T(8,128)S(1)} %fusion.39, s32[2048]{0:T(1024)S(1)} %bitcast.108), kind=kOutput, calls=%fused_computation.16 | convolution fusion | flops 1611661312 | bytes 4464640 | tf_op jit(solution)/shard_map/dot_general | solution.py:14
  22.0 3.6 %fusion.7 = bf16[2048,128]{1,0:T(8,128)(2,1)S(1)} fusion(f32[256,2048]{1,0:T(8,128)S(1)} %fusion.10, bf16[2048,128]{1,0:T(8,128)(2,1)S(1)} %bitcast.96, bf16[256,128]{1,0:T(8,128)(2,1)S(1)} %copy-done.1, f32[256]{0:T(256)S(1)} %get-tuple-element.253, f32[256]{0:T(256)S(1)} %get-tuple-element.254), kind=kOutput, calls=%fused_computation.13 | convolution fusion | flops 806191104 | bytes 3213312 | tf_op jit(solution)/shard_map/dot_general | solution.py:14
  26.1 2.8 %fusion.69 = (f32[2048]{0:T(1024)S(1)}, f32[2048,256]{0,1:T(8,128)S(1)}) fusion(f32[2048,256]{0,1:T(8,128)S(1)} %fusion.71, f32[256,256]{1,0:T(8,128)S(1)} %fusion.78, f32[256,2048]{1,0:T(8,128)S(1)} %fusion.39, f32[256]{0:T(256)S(1)} %get-tuple-element.253, s32[2048]{0:T(1024)S(1)} %bitcast.109), kind=kOutput, calls=%fused_computation.107 | convolution fusion | flops 1614804992 | bytes 6571008 | tf_op jit(solution)/shard_map/dot_general | solution.py:14
  29.2 0.5 fusion.14
  29.8 30.3 %while.21 = (s32[]{:T(128)}, f32[2048,1]{0,1:T(1,128)S(1)}, f32[2048,1]{0,1:T(1,128)S(1)}, f32[2048,128]{1,0:T(8,128)S(1)}, bf16[256,128]{1,0:T(8,128)(2,1)S(1)}...) while((s32[]{:T(128)}, f32[2048,1]{0,1:T(1,128)S(1)}, ...), condition=%wide.region_8.9_spmd, body=%wide.region_3.8_spmd.sunk | while | flops 322441216 | bytes 10027399 | solution.py:143
  29.8 1.9 %collective-permute-start.1 = (bf16[256,128]{1,0:T(8,128)(2,1)S(1)}, bf16[256,128]{1,0:T(8,128)(2,1)S(1)}, u32[]{:S(2)}, u32[]{:S(2)}) collective-permute-start(bf16[256,128]{1,0:T(8,128)(2,1)S(1)} %get-tuple-element.353), channel_id=1, source_target_pairs={{0,1},{1,2},{2,3},{3,4},{4,5},{5,6},{6,7},{7,8},{8,9},{9,10},{10,1... | collective-permute-start | bytes 196616 | tf_op jit(solution)/shard_map/while/body/eval_jaxpr/ppermute | solution.py:10
  31.7 3.5 %collective-permute-start = (bf16[256,128]{1,0:T(8,128)(2,1)S(1)}, bf16[256,128]{1,0:T(8,128)(2,1)S(1)}, u32[]{:S(2)}, u32[]{:S(2)}) collective-permute-start(bf16[256,128]{1,0:T(8,128)(2,1)S(1)} %get-tuple-element.352), channel_id=1, source_target_pairs={{0,1},{1,2},{2,3},{3,4},{4,5},{5,6},{6,7},{7,8},{8,9},{9,10},{10,1... | collective-permute-start | bytes 196616 | tf_op jit(solution)/shard_map/while/body/eval_jaxpr/ppermute | solution.py:10
  35.3 0.6 dynamic_slice.12
  37.2 1.9 %collective-permute-done = bf16[256,128]{1,0:T(8,128)(2,1)S(1)} collective-permute-done((bf16[256,128]{1,0:T(8,128)(2,1)S(1)}, bf16[256,128]{1,0:T(8,128)(2,1)S(1)}, u32[]{:S(2)}, u32[]{:S(2)}) %collective-permute-start) | collective-permute-done | bytes 65568 | tf_op jit(solution)/shard_map/while/body/eval_jaxpr/ppermute | solution.py:10
  39.1 1.6 %conditional.2 = ((f32[2048,1]{0,1:T(1,128)S(1)}, f32[2048,1]{0,1:T(1,128)S(1)}, f32[2048,128]{1,0:T(8,128)S(1)})) conditional(s32[]{:T(128)} %convert_element_type.157, (f32[2048,1]{0,1:T(1,128)S(1)}, f32[2048,1]{0,1:T(1,128)S(1)}, f32[2048,128]{1,0:T(8,128)S(1)}) %tuple.41, (bf16[256,128]{1,0:T(8,128)(2,1)S(1)}, bf16[2048,128]{1,0:T(8,128)(2,1)S(1)}, ...), branch_computations={%region_4.4_spmd, %region_5.7_spmd} | conditional | flops 272109568 | bytes 9175072 | solution.py:132
  39.1 0.4 fusion.68
  39.9 0.8 %convolution_add_fusion = f32[2048,128]{1,0:T(8,128)S(1)} fusion(bf16[256,128]{1,0:T(8,128)(2,1)S(1)} %get-tuple-element.205, f32[2048,256]{0,1:T(8,128)S(1)} %get-tuple-element.250, f32[2048,128]{1,0:T(8,128)S(1)} %get-tuple-element.204, f32[2048]{0:T(1024)S(1)} %bitcast.99, f32[2048]{0:T(1024)S(1)} %bitcast.104), kind=kOutput, calls=%fused_computation.1 | convolution fusion | flops 135790592 | bytes 4276224 | tf_op jit(solution)/shard_map/while/body/eval_jaxpr/cond/branch_1_fun/dot_general | solution.py:104
  41.0 1.9 %collective-permute-start.1 = (bf16[256,128]{1,0:T(8,128)(2,1)S(1)}, bf16[256,128]{1,0:T(8,128)(2,1)S(1)}, u32[]{:S(2)}, u32[]{:S(2)}) collective-permute-start(bf16[256,128]{1,0:T(8,128)(2,1)S(1)} %get-tuple-element.353), channel_id=1, source_target_pairs={{0,1},{1,2},{2,3},{3,4},{4,5},{5,6},{6,7},{7,8},{8,9},{9,10},{10,1... | collective-permute-start | bytes 196616 | tf_op jit(solution)/shard_map/while/body/eval_jaxpr/ppermute | solution.py:10
  42.9 1.9 %collective-permute-start = (bf16[256,128]{1,0:T(8,128)(2,1)S(1)}, bf16[256,128]{1,0:T(8,128)(2,1)S(1)}, u32[]{:S(2)}, u32[]{:S(2)}) collective-permute-start(bf16[256,128]{1,0:T(8,128)(2,1)S(1)} %get-tuple-element.352), channel_id=1, source_target_pairs={{0,1},{1,2},{2,3},{3,4},{4,5},{5,6},{6,7},{7,8},{8,9},{9,10},{10,1... | collective-permute-start | bytes 196616 | tf_op jit(solution)/shard_map/while/body/eval_jaxpr/ppermute | solution.py:10
  44.9 0.6 dynamic_slice.12
  46.7 1.7 %collective-permute-done.1 = bf16[256,128]{1,0:T(8,128)(2,1)S(1)} collective-permute-done((bf16[256,128]{1,0:T(8,128)(2,1)S(1)}, bf16[256,128]{1,0:T(8,128)(2,1)S(1)}, u32[]{:S(2)}, u32[]{:S(2)}) %collective-permute-start.1) | collective-permute-done | bytes 65568 | tf_op jit(solution)/shard_map/while/body/eval_jaxpr/ppermute | solution.py:10
  48.4 1.9 %collective-permute-done = bf16[256,128]{1,0:T(8,128)(2,1)S(1)} collective-permute-done((bf16[256,128]{1,0:T(8,128)(2,1)S(1)}, bf16[256,128]{1,0:T(8,128)(2,1)S(1)}, u32[]{:S(2)}, u32[]{:S(2)}) %collective-permute-start) | collective-permute-done | bytes 65568 | tf_op jit(solution)/shard_map/while/body/eval_jaxpr/ppermute | solution.py:10
  50.6 1.9 %collective-permute-start.1 = (bf16[256,128]{1,0:T(8,128)(2,1)S(1)}, bf16[256,128]{1,0:T(8,128)(2,1)S(1)}, u32[]{:S(2)}, u32[]{:S(2)}) collective-permute-start(bf16[256,128]{1,0:T(8,128)(2,1)S(1)} %get-tuple-element.353), channel_id=1, source_target_pairs={{0,1},{1,2},{2,3},{3,4},{4,5},{5,6},{6,7},{7,8},{8,9},{9,10},{10,1... | collective-permute-start | bytes 196616 | tf_op jit(solution)/shard_map/while/body/eval_jaxpr/ppermute | solution.py:10
  52.5 1.9 %collective-permute-start = (bf16[256,128]{1,0:T(8,128)(2,1)S(1)}, bf16[256,128]{1,0:T(8,128)(2,1)S(1)}, u32[]{:S(2)}, u32[]{:S(2)}) collective-permute-start(bf16[256,128]{1,0:T(8,128)(2,1)S(1)} %get-tuple-element.352), channel_id=1, source_target_pairs={{0,1},{1,2},{2,3},{3,4},{4,5},{5,6},{6,7},{7,8},{8,9},{9,10},{10,1... | collective-permute-start | bytes 196616 | tf_op jit(solution)/shard_map/while/body/eval_jaxpr/ppermute | solution.py:10
  54.5 0.6 dynamic_slice.12
  56.3 1.7 %collective-permute-done.1 = bf16[256,128]{1,0:T(8,128)(2,1)S(1)} collective-permute-done((bf16[256,128]{1,0:T(8,128)(2,1)S(1)}, bf16[256,128]{1,0:T(8,128)(2,1)S(1)}, u32[]{:S(2)}, u32[]{:S(2)}) %collective-permute-start.1) | collective-permute-done | bytes 65568 | tf_op jit(solution)/shard_map/while/body/eval_jaxpr/ppermute | solution.py:10
  58.0 1.9 %collective-permute-done = bf16[256,128]{1,0:T(8,128)(2,1)S(1)} collective-permute-done((bf16[256,128]{1,0:T(8,128)(2,1)S(1)}, bf16[256,128]{1,0:T(8,128)(2,1)S(1)}, u32[]{:S(2)}, u32[]{:S(2)}) %collective-permute-start) | collective-permute-done | bytes 65568 | tf_op jit(solution)/shard_map/while/body/eval_jaxpr/ppermute | solution.py:10
  60.9 0.9 %copy.14 = bf16[32,8,8,128]{3,1,2,0:T(8,128)(2,1)} copy(bf16[32,8,8,128]{3,2,1,0:T(8,128)(2,1)S(1)} %bitcast.101) | data formatting | bytes 1048576
  (58 shorter events, 14.4 us)
Async XLA Ops:
  0.0 18.8 %copy-start = (bf16[256,1024]{1,0:T(8,128)(2,1)S(1)}, bf16[256,1024]{1,0:T(8,128)(2,1)}, u32[]{:S(2)}) copy-start(bf16[256,1024]{1,0:T(8,128)(2,1)} %param.10) | copy-start | bytes 1572868
  14.3 2.0 %copy-start.1 = (bf16[256,128]{1,0:T(8,128)(2,1)S(1)}, bf16[256,128]{1,0:T(8,128)(2,1)}, u32[]{:S(2)}) copy-start(bf16[256,128]{1,0:T(8,128)(2,1)} %param.13) | copy-start | bytes 196612
  14.7 2.5 %copy-start.2 = (bf16[256,128]{1,0:T(8,128)(2,1)S(1)}, bf16[256,128]{1,0:T(8,128)(2,1)}, u32[]{:S(2)}) copy-start(bf16[256,128]{1,0:T(8,128)(2,1)} %param.11) | copy-start | bytes 196612
  29.2 0.7 %copy-start.3 = (s32[32]{0:T(128)S(1)}, s32[32]{0:T(128)}, u32[]{:S(2)}) copy-start(s32[32]{0:T(128)} %param.15) | copy-start | bytes 388
  29.8 7.4 %collective-permute-start.1 = (bf16[256,128]{1,0:T(8,128)(2,1)S(1)}, bf16[256,128]{1,0:T(8,128)(2,1)S(1)}, u32[]{:S(2)}, u32[]{:S(2)}) collective-permute-start(bf16[256,128]{1,0:T(8,128)(2,1)S(1)} %get-tuple-element.353), channel_id=1, source_target_pairs={{0,1},{1,2},{2,3},{3,4},{4,5},{5,6},{6,7},{7,8},{8,9},{9,10},{10,1... | collective-permute-start | bytes 196616 | tf_op jit(solution)/shard_map/while/body/eval_jaxpr/ppermute | solution.py:10
  31.7 7.4 %collective-permute-start = (bf16[256,128]{1,0:T(8,128)(2,1)S(1)}, bf16[256,128]{1,0:T(8,128)(2,1)S(1)}, u32[]{:S(2)}, u32[]{:S(2)}) collective-permute-start(bf16[256,128]{1,0:T(8,128)(2,1)S(1)} %get-tuple-element.352), channel_id=1, source_target_pairs={{0,1},{1,2},{2,3},{3,4},{4,5},{5,6},{6,7},{7,8},{8,9},{9,10},{10,1... | collective-permute-start | bytes 196616 | tf_op jit(solution)/shard_map/while/body/eval_jaxpr/ppermute | solution.py:10
  41.0 7.4 %collective-permute-start.1 = (bf16[256,128]{1,0:T(8,128)(2,1)S(1)}, bf16[256,128]{1,0:T(8,128)(2,1)S(1)}, u32[]{:S(2)}, u32[]{:S(2)}) collective-permute-start(bf16[256,128]{1,0:T(8,128)(2,1)S(1)} %get-tuple-element.353), channel_id=1, source_target_pairs={{0,1},{1,2},{2,3},{3,4},{4,5},{5,6},{6,7},{7,8},{8,9},{9,10},{10,1... | collective-permute-start | bytes 196616 | tf_op jit(solution)/shard_map/while/body/eval_jaxpr/ppermute | solution.py:10
  42.9 7.4 %collective-permute-start = (bf16[256,128]{1,0:T(8,128)(2,1)S(1)}, bf16[256,128]{1,0:T(8,128)(2,1)S(1)}, u32[]{:S(2)}, u32[]{:S(2)}) collective-permute-start(bf16[256,128]{1,0:T(8,128)(2,1)S(1)} %get-tuple-element.352), channel_id=1, source_target_pairs={{0,1},{1,2},{2,3},{3,4},{4,5},{5,6},{6,7},{7,8},{8,9},{9,10},{10,1... | collective-permute-start | bytes 196616 | tf_op jit(solution)/shard_map/while/body/eval_jaxpr/ppermute | solution.py:10
  50.6 7.4 %collective-permute-start.1 = (bf16[256,128]{1,0:T(8,128)(2,1)S(1)}, bf16[256,128]{1,0:T(8,128)(2,1)S(1)}, u32[]{:S(2)}, u32[]{:S(2)}) collective-permute-start(bf16[256,128]{1,0:T(8,128)(2,1)S(1)} %get-tuple-element.353), channel_id=1, source_target_pairs={{0,1},{1,2},{2,3},{3,4},{4,5},{5,6},{6,7},{7,8},{8,9},{9,10},{10,1... | collective-permute-start | bytes 196616 | tf_op jit(solution)/shard_map/while/body/eval_jaxpr/ppermute | solution.py:10
  52.5 7.4 %collective-permute-start = (bf16[256,128]{1,0:T(8,128)(2,1)S(1)}, bf16[256,128]{1,0:T(8,128)(2,1)S(1)}, u32[]{:S(2)}, u32[]{:S(2)}) collective-permute-start(bf16[256,128]{1,0:T(8,128)(2,1)S(1)} %get-tuple-element.352), channel_id=1, source_target_pairs={{0,1},{1,2},{2,3},{3,4},{4,5},{5,6},{6,7},{7,8},{8,9},{9,10},{10,1... | collective-permute-start | bytes 196616 | tf_op jit(solution)/shard_map/while/body/eval_jaxpr/ppermute | solution.py:10
where the time goes:
time: 62.2 us; the launch traced here: 61.8 us
  matrix products  27.1 us (44%)
  starting transfers between devices  13.1 us (21%)
  waiting for transfers between devices  9.27 us (15%)
  local copies, waits for them, and re-layouts  5.45 us (9%)
  loops' own time  3.8 us (6%)
  other arithmetic  2.65 us (4%)
    dot_general x35, matrix products, matmul(): jnp.dot(left_side, right_side, precision=lax.Precision.HIGHEST, preferred...  21.5 us
    ppermute x6, starting transfers between devices, passed_along(): lax.ppermute(value, axis, [(source, source + steps) for source in range(i...  13.1 us
    ppermute x6, waiting for transfers between devices, passed_along(): lax.ppermute(value, axis, [(source, source + steps) for source in range(i...  9.27 us
    another operation x1, loops' own time, local(): lax.fori_loop(1, longest, chain_step, (softmax_state, key_end, values))  3.77 us
    dot_general x6, matrix products, apply_map(): lax.dot_general(vectors, matrix, (((1,), (1,)), ((), ())), precision=lax....  3.4 us
    unnamed x12, local copies, waits for them, and re-layouts  1.93 us
    dynamic_slice x3, local copies, waits for them, and re-layouts, visit(): doc_of_block[jnp.clip(source, 0, last_block)] == own_doc  1.84 us
  transfers between devices with their start and end apart: 6, of which 6 were waited for; matrix products, arithmetic and copies ran while one was open for 3% of the time, Pallas kernels for 0%

commit v1 on v0

v1 whole, which is shorter than its diff:
```python
import functools
import math

import jax
import jax.numpy as jnp
from jax import lax
from jax.experimental import pallas as pl
from jax.experimental.pallas import tpu as pltpu
from jax.sharding import PartitionSpec as P

F32 = jnp.float32
BF16 = jnp.bfloat16
AXES = ("outer", "inner")
GROUP = 3
VMEM_LIMIT = 48 * 1024 * 1024


def dot(left, right):
    return jnp.dot(left, right, preferred_element_type=F32)


def dot_rows(left, right):
    return lax.dot_general(left, right, (((1,), (1,)), ((), ())), preferred_element_type=F32)


def halves(value):
    high = value.astype(BF16)
    return high, (value - high.astype(F32)).astype(BF16)


def dot_halves(left, right):
    (left_high, left_low), (right_high, right_low) = left, right
    return dot(left_high, right_high) + (dot(left_high, right_low) + dot(left_low, right_high))


def unit_inverses(strict_parts):
    length = strict_parts[0].shape[0]
    rows = lax.broadcasted_iota(jnp.int32, (length, length), 0)
    columns = lax.broadcasted_iota(jnp.int32, (length, length), 1)
    identity = (rows == columns).astype(F32)
    results = [identity - part for part in strict_parts]
    powers = [halves(part) for part in strict_parts]
    reach = 2
    while reach < length:
        powers = [halves(dot_halves(power, power)) for power in powers]
        results = [
            result + dot_halves(halves(result), power) for result, power in zip(results, powers)
        ]
        reach = reach * 2
    return results


def key_kernel(reflect_ref, keys_ref, values_ref, logit_ref, packet_ref, solved_ref, gain_ref):
    reflect = reflect_ref[...]
    keys = keys_ref[...]
    length, head_size = reflect.shape
    half = length // 2
    reflect_float = reflect.astype(F32)
    square_high, square_low = halves(reflect_float * reflect_float)
    ones = jnp.ones((8, head_size), BF16)
    norms = dot_rows(ones, square_high) + dot_rows(ones, square_low)
    strength = 2.0 / (1.0 + jnp.exp(-logit_ref[...]))
    gains = strength / (norms + 1e-06)
    gain_ref[...] = gains
    gain = gains[0:1, :]
    rows = lax.broadcasted_iota(jnp.int32, (length, length), 0)
    columns = lax.broadcasted_iota(jnp.int32, (length, length), 1)
    strictly = rows > columns
    chained = jnp.where(strictly, dot_rows(reflect, reflect) * gain, 0.0)
    facing = jnp.where(strictly, dot_rows(reflect, keys), 0.0)
    reflect_turned = reflect_float.T
    keys_turned = keys.astype(F32).T
    scaled = halves(reflect_turned * gain)
    first, second = unit_inverses([chained[:half, :half], chained[half:, half:]])
    first, second = halves(first), halves(second)
    wide = jnp.concatenate([facing[:half, :half], reflect_float[:half]], axis=1)
    upper = dot_halves(first, halves(wide))
    tall = jnp.concatenate([facing[half:, :half], reflect_float[half:], facing[half:, half:]], axis=1)
    lower = dot_halves(second, halves(tall))
    bridge = dot_halves(second, halves(chained[half:, :half]))
    cross = dot_halves(halves(bridge), halves(upper))
    lower_left = lower[:, : half + head_size] - cross
    solved = jnp.concatenate(
        [
            jnp.concatenate(
                [upper[:, :half], jnp.zeros((half, half), F32), upper[:, half:]], axis=1
            ),
            jnp.concatenate(
                [lower_left[:, :half], lower[:, half + head_size :], lower_left[:, half:]], axis=1
            ),
        ],
        axis=0,
    )
    solved = halves(solved)
    wide_size = length + head_size
    solved_ref[:, :wide_size] = solved[0]
    solved_ref[:, wide_size:] = solved[1]
    change = dot_halves(scaled, solved)
    head_rows = lax.broadcasted_iota(jnp.int32, (head_size, head_size), 0)
    head_columns = lax.broadcasted_iota(jnp.int32, (head_size, head_size), 1)
    identity = (head_rows == head_columns).astype(F32)
    packet_ref[:, :length] = (keys_turned - change[:, :length]).astype(BF16)
    packet_ref[:, length:wide_size] = (identity - change[:, length:]).astype(BF16)
    for part in range(length // head_size):
        start = wide_size + part * head_size
        packet_ref[:, start : start + head_size] = values_ref[
            part * head_size : (part + 1) * head_size, :
        ]


def query_kernel(
    head_count,
    queries_ref,
    reflect_ref,
    keys_ref,
    values_ref,
    solved_ref,
    gain_ref,
    turned_ref,
    peak_ref,
    total_ref,
    weighted_ref,
):
    length, head_size = keys_ref.shape
    wide_size = length + head_size
    rate = math.log2(math.e) * head_size ** (-0.5)
    rows = lax.broadcasted_iota(jnp.int32, (length, length), 0)
    columns = lax.broadcasted_iota(jnp.int32, (length, length), 1)
    visible = rows >= columns
    gain = jnp.where(visible, gain_ref[0:1, :], 0.0)
    hidden = jnp.where(visible, 0.0, -1e30)
    both = jnp.concatenate([reflect_ref[...], keys_ref[...]], axis=0)
    solved_high = solved_ref[:, :wide_size]
    solved_low = solved_ref[:, wide_size:]
    values = values_ref[...]
    for head in range(head_count):
        span = slice(head * head_size, (head + 1) * head_size)
        queries = queries_ref[:, span]
        faced = dot_rows(queries, both)
        change = dot_halves(halves(faced[:, :length] * gain), (solved_high, solved_low))
        scores = (faced[:, length:] - change[:, :length]) + hidden
        turned_ref[:, span] = (queries.astype(F32) - change[:, length:]).astype(BF16)
        peak = jnp.max(scores, axis=1, keepdims=True)
        weights = jnp.exp2((scores - peak) * rate)
        total = jnp.sum(weights, axis=1, keepdims=True)
        weighted_ref[:, span] = dot(weights.astype(BF16), values)
        peak_ref[:, span] = jnp.broadcast_to(peak, (length, head_size))
        total_ref[:, span] = jnp.broadcast_to(total, (length, head_size))


def earlier_kernel(head_count, longest, docs_ref, *refs):
    packet_refs = refs[: longest - 1]
    turned_ref, peak_ref, total_ref, weighted_ref, out_ref, keys_ref, values_ref = refs[longest - 1 :]
    length = turned_ref.shape[0]
    head_size = turned_ref.shape[1] // head_count
    wide_size = length + head_size
    rate = math.log2(math.e) * head_size ** (-0.5)
    block = lax.axis_index("outer") * lax.axis_size("inner") + lax.axis_index("inner")
    own_doc = docs_ref[block]
    present = jnp.int32(0)
    for distance in range(1, longest):
        source = block - distance
        same = (source >= 0) & (docs_ref[jnp.maximum(source, 0)] == own_doc)
        present = present + same.astype(jnp.int32)
    odd = (block % 2) == 1
    steps = longest // 2 - 1
    apart_refs, swapped_refs, mixed_ref = (
        packet_refs[:steps],
        packet_refs[steps : 2 * steps],
        packet_refs[2 * steps],
    )
    transit = None
    for distance in range(1, longest):
        if distance % 2 == 0:
            packet = apart_refs[distance // 2 - 1][...]
        else:
            odd_ref = mixed_ref if distance == 1 else swapped_refs[(distance - 1) // 2 - 1]
            even_ref = mixed_ref if distance == longest - 1 else swapped_refs[(distance + 1) // 2 - 1]
            packet = jnp.where(odd, odd_ref[...], even_ref[...])
        keys = packet[:, :length]
        own_transit = packet[:, length:wide_size]
        slot, place = (distance - 1) // GROUP, (distance - 1) % GROUP
        if distance == 1:
            transit = own_transit.astype(F32)
        elif distance == 2:
            first = transit.astype(BF16)
            keys = dot(first, keys).astype(BF16)
            transit = dot(first, own_transit)
        else:
            high, low = halves(transit)
            keys = (dot(high, keys) + dot(low, keys)).astype(BF16)
            if distance < longest - 1:
                transit = dot(high, own_transit) + dot(low, own_transit)
        keys_ref[slot, :, place * length : (place + 1) * length] = keys
        for part in range(length // head_size):
            start = wide_size + part * head_size
            row = place * length + part * head_size
            values_ref[slot, row : row + head_size, :] = packet[:, start : start + head_size]
    slots = keys_ref.shape[0]
    for extra in range(longest - 1, slots * GROUP):
        slot, place = extra // GROUP, extra % GROUP
        keys_ref[slot, :, place * length : (place + 1) * length] = jnp.zeros(
            (head_size, length), BF16
        )
        values_ref[slot, place * length : (place + 1) * length, :] = jnp.zeros(
            (length, head_size), BF16
        )
    spot = lax.broadcasted_iota(jnp.int32, (1, GROUP * length), 1)

    def visit(slot):
        hidden = jnp.where(spot < (present - slot * GROUP) * length, 0.0, -1e30)
        keys = keys_ref[slot]
        values = values_ref[slot]
        for head in range(head_count):
            span = slice(head * head_size, (head + 1) * head_size)
            scores = dot(turned_ref[:, span], keys) + hidden
            old_peak = peak_ref[:, span][:, 0:1]
            peak = jnp.maximum(old_peak, jnp.max(scores, axis=1, keepdims=True))
            weights = jnp.exp2((scores - peak) * rate)
            factor = jnp.exp2((old_peak - peak) * rate)
            total = total_ref[:, span][:, 0:1] * factor + jnp.sum(weights, axis=1, keepdims=True)
            weighted = weighted_ref[:, span] * factor + dot(weights.astype(BF16), values)
            if slots == 1:
                out_ref[:, span] = (weighted / total).astype(BF16)
            else:
                peak_ref[:, span] = jnp.broadcast_to(peak, (length, head_size))
                total_ref[:, span] = jnp.broadcast_to(total, (length, head_size))
                weighted_ref[:, span] = weighted

    def finish():
        for head in range(head_count):
            span = slice(head * head_size, (head + 1) * head_size)
            out_ref[:, span] = (weighted_ref[:, span] / total_ref[:, span]).astype(BF16)

    if slots == 1:
        visit(0)
    else:
        @pl.loop(0, (present + GROUP - 1) // GROUP)
        def _(slot):
            visit(slot)

        finish()


def vmem(count):
    return [pl.BlockSpec(memory_space=pltpu.VMEM)] * count


def permuted(value, target):
    count = lax.axis_size("outer") * lax.axis_size("inner")
    return lax.ppermute(value, AXES, [(i, target(i) % count) for i in range(count)])


def local(queries, keys, values, reflect, reflect_logit, doc_of_block):
    longest = lax.axis_size("outer") * lax.axis_size("inner") // 8
    length, head_size = keys.shape
    head_count = queries.shape[1] // head_size
    wide_size = length + head_size
    params = pltpu.CompilerParams(vmem_limit_bytes=VMEM_LIMIT)
    packet, solved, gain = pl.pallas_call(
        key_kernel,
        out_shape=(
            jax.ShapeDtypeStruct((head_size, wide_size + length), BF16),
            jax.ShapeDtypeStruct((length, 2 * wide_size), BF16),
            jax.ShapeDtypeStruct((8, length), F32),
        ),
        in_specs=vmem(4),
        out_specs=tuple(vmem(3)),
        compiler_params=params,
        cost_estimate=pl.CostEstimate(
            flops=40 * length**3, bytes_accessed=8 * length * length, transcendentals=length
        ),
        name="key_side",
    )(reflect, keys, values, reflect_logit.reshape(1, length))
    apart = [permuted(packet, lambda i, s=s: i + 2 * s) for s in range(1, longest // 2)]
    mixed = permuted(packet, lambda i: i + longest - 1 if i % 2 else i + 1)
    swapped = [permuted(moved, lambda i: i ^ 1) for moved in apart]
    wide = jax.ShapeDtypeStruct(queries.shape, F32)
    turned, peak, total, weighted = pl.pallas_call(
        functools.partial(query_kernel, head_count),
        out_shape=(jax.ShapeDtypeStruct(queries.shape, BF16), wide, wide, wide),
        in_specs=vmem(6),
        out_specs=tuple(vmem(4)),
        compiler_params=params,
        cost_estimate=pl.CostEstimate(
            flops=head_count * 10 * length**3,
            bytes_accessed=16 * length * length * head_count,
            transcendentals=head_count * length * length,
        ),
        name="query_side",
    )(queries, reflect, keys, values, solved, gain)
    slots = (longest - 1 + GROUP - 1) // GROUP
    return pl.pallas_call(
        functools.partial(earlier_kernel, head_count, longest),
        out_shape=jax.ShapeDtypeStruct(queries.shape, BF16),
        in_specs=[pl.BlockSpec(memory_space=pltpu.SMEM)] + vmem(longest - 1 + 4),
        out_specs=vmem(1)[0],
        scratch_shapes=[
            pltpu.VMEM((slots, head_size, GROUP * length), BF16),
            pltpu.VMEM((slots, GROUP * length, head_size), BF16),
        ],
        compiler_params=params,
        cost_estimate=pl.CostEstimate(
            flops=head_count * 6 * length**3,
            bytes_accessed=16 * length * length * head_count,
            transcendentals=3 * head_count * length * length,
        ),
        name="earlier_blocks",
    )(doc_of_block, *apart, *swapped, mixed, turned, peak, total, weighted)


def solution(mesh):
    placed = (
        P(AXES, None),
        P(AXES, None),
        P(AXES, None),
        P(AXES, None),
        P(AXES),
        P(),
    )
    return jax.shard_map(
        local, mesh=mesh, in_specs=placed, out_specs=P(AXES, None), check_vma=False
    )
```

time: 62.2 us -> 28.3 us (0.45)
  the two profiles are of different devices: /device:TPU:8 before, /device:TPU:1 now
where the time goes in v1:
time: 28.3 us; the launch traced here: 28 us
  Pallas kernels  12 us (42%)
  starting transfers between devices  6.26 us (22%)
  waiting for transfers between devices  5.82 us (21%)
  local copies, waits for them, and re-layouts  3.85 us (14%)
    ppermute x3, starting transfers between devices, permuted(): lax.ppermute(value, AXES, [(i, target(i) % count) for i in range(count)])  6.26 us
    pallas_call x1, Pallas kernels, local(): pl.pallas_call(functools.partial(earlier_kernel, head_count, longest), ou...  5.98 us
    ppermute x3, waiting for transfers between devices, permuted(): lax.ppermute(value, AXES, [(i, target(i) % count) for i in range(count)])  5.82 us
    unnamed x12, local copies, waits for them, and re-layouts  3.85 us
    pallas_call x1, Pallas kernels, local(): pl.pallas_call(functools.partial(query_kernel, head_count), out_shape=(ja...  3.55 us
    pallas_call x1, Pallas kernels, local(): pl.pallas_call(key_kernel, out_shape=(jax.ShapeDtypeStruct((head_size, wi...  2.49 us
  transfers between devices with their start and end apart: 3, of which 1 were waited for; matrix products, arithmetic and copies ran while one was open for 0% of the time, Pallas kernels for 13%

profile of v1, /device:TPU:1, one launch (start us, length us, event | category | flops | bytes accessed | tf_op | source)
XLA Modules:
  0.0 28.0 jit_solution(7551065731992914151)
XLA Ops:
  0.0 0.0 copy-start.5
  0.0 0.7 %copy-done.5 = f32[256]{0:T(256)S(1)} copy-done((f32[256]{0:T(256)S(1)}, f32[256]{0:T(256)}, u32[]{:S(2)}) %copy-start.5) | copy-done | bytes 1048
  0.7 0.0 copy-start.2
  0.7 0.8 %copy-done.2 = bf16[256,128]{1,0:T(8,128)(2,1)S(1)} copy-done((bf16[256,128]{1,0:T(8,128)(2,1)S(1)}, bf16[256,128]{1,0:T(8,128)(2,1)}, u32[]{:S(2)}) %copy-start.2) | copy-done | bytes 65560
  1.5 0.0 copy-start.3
  1.5 0.8 %copy-done.3 = bf16[256,128]{1,0:T(8,128)(2,1)S(1)} copy-done((bf16[256,128]{1,0:T(8,128)(2,1)S(1)}, bf16[256,128]{1,0:T(8,128)(2,1)}, u32[]{:S(2)}) %copy-start.3) | copy-done | bytes 65560
  2.4 0.0 copy-start.4
  2.4 0.8 %copy-done.4 = bf16[256,128]{1,0:T(8,128)(2,1)S(1)} copy-done((bf16[256,128]{1,0:T(8,128)(2,1)S(1)}, bf16[256,128]{1,0:T(8,128)(2,1)}, u32[]{:S(2)}) %copy-start.4) | copy-done | bytes 65560
  3.2 0.0 copy-start.1
  3.2 2.5 %key_side.1 = (bf16[128,640]{1,0:T(8,128)(2,1)S(1)}, bf16[256,768]{1,0:T(8,128)(2,1)S(1)}, f32[8,256]{1,0:T(8,128)S(1)}) custom-call(bf16[256,128]{1,0:T(8,128)(2,1)S(1)} %copy-done.2, bf16[256,128]{1,0:T(8,128)(2,1)S(1)} %copy-done.3, bf16[256,128]{1,0:T(8,128)(2,1)S(1)} %copy-done.4, f32[1,256]{1,0:T(1,128)S(1)} %bitcast.1), custom_call_target="tpu_custom_call" | custom-call | flops 671088640 | bytes 524288 | tf_op jit(solution)/shard_map/key_side/pallas_call | solution.py:260
  5.7 2.1 %collective-permute-start = (bf16[128,640]{1,0:T(8,128)(2,1)S(1)}, bf16[128,640]{1,0:T(8,128)(2,1)S(1)}, u32[]{:S(2)}, u32[]{:S(2)}) collective-permute-start(bf16[128,640]{1,0:T(8,128)(2,1)S(1)} %get-tuple-element.12), channel_id=1, source_target_pairs={{0,2},{1,3},{2,4},{3,5},{4,6},{5,7},{6,8},{7,9},{8,10},{9,11},{10,... | collective-permute-start | bytes 491528 | tf_op jit(solution)/shard_map/ppermute | solution.py:251
  7.8 2.1 %collective-permute-start.2 = (bf16[128,640]{1,0:T(8,128)(2,1)S(1)}, bf16[128,640]{1,0:T(8,128)(2,1)S(1)}, u32[]{:S(2)}, u32[]{:S(2)}) collective-permute-start(bf16[128,640]{1,0:T(8,128)(2,1)S(1)} %get-tuple-element.12), channel_id=1, source_target_pairs={{0,1},{1,4},{2,3},{3,6},{4,5},{5,8},{6,7},{7,10},{8,9},{9,12},{10,... | collective-permute-start | bytes 491528 | tf_op jit(solution)/shard_map/ppermute | solution.py:251
  9.9 5.8 %collective-permute-done.refs_0_ = bf16[128,640]{1,0:T(8,128)(2,1)S(1)} collective-permute-done((bf16[128,640]{1,0:T(8,128)(2,1)S(1)}, bf16[128,640]{1,0:T(8,128)(2,1)S(1)}, u32[]{:S(2)}, u32[]{:S(2)}) %collective-permute-start) | collective-permute-done | bytes 163872 | tf_op jit(solution)/shard_map/ppermute | solution.py:251
  15.7 2.1 %collective-permute-start.1 = (bf16[128,640]{1,0:T(8,128)(2,1)S(1)}, bf16[128,640]{1,0:T(8,128)(2,1)S(1)}, u32[]{:S(2)}, u32[]{:S(2)}) collective-permute-start(bf16[128,640]{1,0:T(8,128)(2,1)S(1)} %collective-permute-done.refs_0_), channel_id=1, source_target_pairs={{0,1},{1,0},{2,3},{3,2},{4,5},{5,4},{6,7},{7,6},{8,9},{9,8},{10,11... | collective-permute-start | bytes 491528 | tf_op jit(solution)/shard_map/ppermute | solution.py:251
  17.8 0.0 copy-done.1
  17.8 3.6 %query_side.1 = (bf16[256,1024]{1,0:T(8,128)(2,1)S(1)}, f32[256,1024]{1,0:T(8,128)S(1)}, f32[256,1024]{1,0:T(8,128)S(1)}, f32[256,1024]{1,0:T(8,128)S(1)}) custom-call(bf16[256,1024]{1,0:T(8,128)(2,1)S(1)} %copy-done.1, bf16[256,128]{1,0:T(8,128)(2,1)S(1)} %copy-done.2, bf16[256,128]{1,0:T(8,128)(2,1)S(1)} %copy-done.3, bf16[256,128]{1,0:T(8,128)(2,1)S(1)} %copy-done.4, ...), custom_call_target="tpu_custom_call" | custom-call | flops 1342177280 | bytes 8388608 | tf_op jit(solution)/shard_map/query_side/pallas_call | solution.py:279
  21.3 0.0 collective-permute-done.2.refs_2_
  21.3 0.0 collective-permute-done.1.refs_1_
  21.4 0.0 copy-start
  21.4 0.6 %copy-done = s32[32]{0:T(128)S(1)} copy-done((s32[32]{0:T(128)S(1)}, s32[32]{0:T(128)}, u32[]{:S(2)}) %copy-start) | copy-done | bytes 152
  22.0 6.0 %earlier_blocks.1 = bf16[256,1024]{1,0:T(8,128)(2,1)} custom-call(s32[32]{0:T(128)S(1)} %copy-done, bf16[128,640]{1,0:T(8,128)(2,1)S(1)} %collective-permute-done.refs_0_, bf16[128,640]{1,0:T(8,128)(2,1)S(1)} %collective-permute-done.1.refs_1_, bf16[128,640]{1,0:T(8,128)(2,1)S(1)} %collective-permute-done.2.refs_2_, ...), custom_call_target="tpu_custom_call" | custom-call | flops 805306368 | bytes 8388608 | tf_op jit(solution)/shard_map/earlier_blocks/pallas_call | solution.py:293
Async XLA Ops:
  0.0 0.7 %copy-start.5 = (f32[256]{0:T(256)S(1)}, f32[256]{0:T(256)}, u32[]{:S(2)}) copy-start(f32[256]{0:T(256)} %param.10) | copy-start | bytes 3076
  0.7 0.8 %copy-start.2 = (bf16[256,128]{1,0:T(8,128)(2,1)S(1)}, bf16[256,128]{1,0:T(8,128)(2,1)}, u32[]{:S(2)}) copy-start(bf16[256,128]{1,0:T(8,128)(2,1)} %reflect_ref.3) | copy-start | bytes 196612
  1.5 0.8 %copy-start.3 = (bf16[256,128]{1,0:T(8,128)(2,1)S(1)}, bf16[256,128]{1,0:T(8,128)(2,1)}, u32[]{:S(2)}) copy-start(bf16[256,128]{1,0:T(8,128)(2,1)} %keys_ref.3) | copy-start | bytes 196612
  2.4 0.8 %copy-start.4 = (bf16[256,128]{1,0:T(8,128)(2,1)S(1)}, bf16[256,128]{1,0:T(8,128)(2,1)}, u32[]{:S(2)}) copy-start(bf16[256,128]{1,0:T(8,128)(2,1)} %values_ref.3) | copy-start | bytes 196612
  3.2 14.6 %copy-start.1 = (bf16[256,1024]{1,0:T(8,128)(2,1)S(1)}, bf16[256,1024]{1,0:T(8,128)(2,1)}, u32[]{:S(2)}) copy-start(bf16[256,1024]{1,0:T(8,128)(2,1)} %queries_ref.1) | copy-start | bytes 1572868
  5.7 10.0 %collective-permute-start = (bf16[128,640]{1,0:T(8,128)(2,1)S(1)}, bf16[128,640]{1,0:T(8,128)(2,1)S(1)}, u32[]{:S(2)}, u32[]{:S(2)}) collective-permute-start(bf16[128,640]{1,0:T(8,128)(2,1)S(1)} %get-tuple-element.12), channel_id=1, source_target_pairs={{0,2},{1,3},{2,4},{3,5},{4,6},{5,7},{6,8},{7,9},{8,10},{9,11},{10,... | collective-permute-start | bytes 491528 | tf_op jit(solution)/shard_map/ppermute | solution.py:251
  7.8 13.5 %collective-permute-start.2 = (bf16[128,640]{1,0:T(8,128)(2,1)S(1)}, bf16[128,640]{1,0:T(8,128)(2,1)S(1)}, u32[]{:S(2)}, u32[]{:S(2)}) collective-permute-start(bf16[128,640]{1,0:T(8,128)(2,1)S(1)} %get-tuple-element.12), channel_id=1, source_target_pairs={{0,1},{1,4},{2,3},{3,6},{4,5},{5,8},{6,7},{7,10},{8,9},{9,12},{10,... | collective-permute-start | bytes 491528 | tf_op jit(solution)/shard_map/ppermute | solution.py:251
  15.7 5.7 %collective-permute-start.1 = (bf16[128,640]{1,0:T(8,128)(2,1)S(1)}, bf16[128,640]{1,0:T(8,128)(2,1)S(1)}, u32[]{:S(2)}, u32[]{:S(2)}) collective-permute-start(bf16[128,640]{1,0:T(8,128)(2,1)S(1)} %collective-permute-done.refs_0_), channel_id=1, source_target_pairs={{0,1},{1,0},{2,3},{3,2},{4,5},{5,4},{6,7},{7,6},{8,9},{9,8},{10,11... | collective-permute-start | bytes 491528 | tf_op jit(solution)/shard_map/ppermute | solution.py:251
  21.4 0.7 %copy-start = (s32[32]{0:T(128)S(1)}, s32[32]{0:T(128)}, u32[]{:S(2)}) copy-start(s32[32]{0:T(128)} %docs_ref.1) | copy-start | bytes 388

commit v2 on v1

v2 whole, which is shorter than its diff:
```python
import functools
import math

import jax
import jax.numpy as jnp
from jax import lax
from jax.experimental import pallas as pl
from jax.experimental.pallas import tpu as pltpu
from jax.sharding import PartitionSpec as P

F32 = jnp.float32
BF16 = jnp.bfloat16
AXES = ("outer", "inner")
GROUP = 3
VMEM_LIMIT = 48 * 1024 * 1024


def dot(left, right):
    return jnp.dot(left, right, preferred_element_type=F32)


def dot_rows(left, right):
    return lax.dot_general(left, right, (((1,), (1,)), ((), ())), preferred_element_type=F32)


def halves(value):
    high = value.astype(BF16)
    return high, (value - high.astype(F32)).astype(BF16)


def dot_halves(left, right):
    (left_high, left_low), (right_high, right_low) = left, right
    return dot(left_high, right_high) + (dot(left_high, right_low) + dot(left_low, right_high))


def unit_inverses(strict_parts):
    length = strict_parts[0].shape[0]
    rows = lax.broadcasted_iota(jnp.int32, (length, length), 0)
    columns = lax.broadcasted_iota(jnp.int32, (length, length), 1)
    identity = (rows == columns).astype(F32)
    results = [identity - part for part in strict_parts]
    powers = [halves(part) for part in strict_parts]
    reach = 2
    while reach < length:
        powers = [halves(dot_halves(power, power)) for power in powers]
        results = [
            result + dot_halves(halves(result), power) for result, power in zip(results, powers)
        ]
        reach = reach * 2
    return results


def key_kernel(
    reflect_hbm,
    keys_hbm,
    values_hbm,
    logit_hbm,
    packet_ref,
    solved_ref,
    gain_ref,
    turned_ref,
    ones_ref,
    reflect_ref,
    keys_ref,
    logit_ref,
    sems,
):
    length, head_size = reflect_ref.shape
    half = length // 2
    wide_size = length + head_size
    copies = [
        pltpu.make_async_copy(reflect_hbm, reflect_ref, sems.at[0]),
        pltpu.make_async_copy(logit_hbm, logit_ref, sems.at[1]),
        pltpu.make_async_copy(keys_hbm, keys_ref, sems.at[2]),
        pltpu.make_async_copy(values_hbm, ones_ref.at[:, pl.ds(0, head_size)], sems.at[3]),
    ]
    for copy in copies:
        copy.start()
    copies[0].wait()
    copies[1].wait()
    reflect = reflect_ref[...]
    reflect_float = reflect.astype(F32)
    square_high, square_low = halves(reflect_float * reflect_float)
    ones = jnp.ones((8, head_size), BF16)
    norms = dot_rows(ones, square_high) + dot_rows(ones, square_low)
    strength = 2.0 / (1.0 + jnp.exp(-logit_ref[...]))
    gains = strength / (norms + 1e-06)
    gain_ref[...] = gains
    gain = gains[0:1, :]
    rows = lax.broadcasted_iota(jnp.int32, (length, length), 0)
    columns = lax.broadcasted_iota(jnp.int32, (length, length), 1)
    strictly = rows > columns
    chained = jnp.where(strictly, dot_rows(reflect, reflect) * gain, 0.0)
    reflect_turned = reflect_float.T
    copies[2].wait()
    keys = keys_ref[...]
    facing = jnp.where(strictly, dot_rows(reflect, keys), 0.0)
    keys_turned = keys.astype(F32).T
    turned_ref[:, :length] = reflect_turned.astype(BF16)
    turned_ref[:, length:] = keys_turned.astype(BF16)
    scaled = halves(reflect_turned * gain)
    first, second = unit_inverses([chained[:half, :half], chained[half:, half:]])
    first, second = halves(first), halves(second)
    wide = jnp.concatenate([facing[:half, :half], reflect_float[:half]], axis=1)
    upper = dot_halves(first, halves(wide))
    tall = jnp.concatenate([facing[half:, :half], reflect_float[half:], facing[half:, half:]], axis=1)
    lower = dot_halves(second, halves(tall))
    bridge = dot_halves(second, halves(chained[half:, :half]))
    cross = dot_halves(halves(bridge), halves(upper))
    lower_left = lower[:, : half + head_size] - cross
    solved = jnp.concatenate(
        [
            jnp.concatenate(
                [upper[:, :half], jnp.zeros((half, half), F32), upper[:, half:]], axis=1
            ),
            jnp.concatenate(
                [lower_left[:, :half], lower[:, half + head_size :], lower_left[:, half:]], axis=1
            ),
        ],
        axis=0,
    )
    solved = halves(solved)
    solved_ref[:, :wide_size] = solved[0]
    solved_ref[:, wide_size:] = solved[1]
    change = dot_halves(scaled, solved)
    head_rows = lax.broadcasted_iota(jnp.int32, (head_size, head_size), 0)
    head_columns = lax.broadcasted_iota(jnp.int32, (head_size, head_size), 1)
    identity = (head_rows == head_columns).astype(F32)
    packet_ref[:, :length] = (keys_turned - change[:, :length]).astype(BF16)
    packet_ref[:, length:wide_size] = (identity - change[:, length:]).astype(BF16)
    copies[3].wait()
    ones_ref[:, head_size:] = jnp.ones((length, head_size), BF16)
    for part in range(length // head_size):
        start = wide_size + part * head_size
        packet_ref[:, start : start + head_size] = ones_ref[
            part * head_size : (part + 1) * head_size, :head_size
        ]


def row_peak(scores, peak):
    size = peak.shape[1]
    pieces = [scores[:, i : i + size] for i in range(0, scores.shape[1], size)]
    return jnp.maximum(peak, jnp.max(functools.reduce(jnp.maximum, pieces), axis=1, keepdims=True))


def row_weights(scores, peak, rate):
    size = peak.shape[1]
    pieces = [
        jnp.exp2((scores[:, i : i + size] - peak) * rate) for i in range(0, scores.shape[1], size)
    ]
    return jnp.concatenate(pieces, axis=1).astype(BF16)


def query_kernel(
    head_count,
    longest,
    docs_hbm,
    queries_ref,
    both_ref,
    ones_ref,
    solved_ref,
    gain_ref,
    turned_ref,
    peak_ref,
    total_ref,
    weighted_ref,
    present_ref,
    docs_ref,
    docs_sem,
):
    docs_copy = pltpu.make_async_copy(docs_hbm, docs_ref, docs_sem)
    docs_copy.start()
    length = ones_ref.shape[0]
    head_size = ones_ref.shape[1] // 2
    wide_size = length + head_size
    rate = math.log2(math.e) * head_size ** (-0.5)
    rows = lax.broadcasted_iota(jnp.int32, (length, length), 0)
    columns = lax.broadcasted_iota(jnp.int32, (length, length), 1)
    visible = rows >= columns
    gain = jnp.where(visible, gain_ref[0:1, :], 0.0)
    hidden = jnp.where(visible, 0.0, -1e30)
    both = both_ref[...]
    solved_high = solved_ref[:, :wide_size]
    solved_low = solved_ref[:, wide_size:]
    values = ones_ref[...]
    for head in range(head_count):
        span = slice(head * head_size, (head + 1) * head_size)
        queries = queries_ref[:, span]
        faced = dot(queries, both)
        change = dot_halves(halves(faced[:, :length] * gain), (solved_high, solved_low))
        scores = (faced[:, length:] - change[:, :length]) + hidden
        turned_ref[:, span] = (queries.astype(F32) - change[:, length:]).astype(BF16)
        peak = jnp.broadcast_to(jnp.max(scores, axis=1, keepdims=True), (length, head_size))
        sums = dot(row_weights(scores, peak, rate), values)
        peak_ref[:, span] = peak
        weighted_ref[:, span] = sums[:, :head_size]
        total_ref[:, span] = sums[:, head_size:]
    docs_copy.wait()
    block = lax.axis_index("outer") * lax.axis_size("inner") + lax.axis_index("inner")
    own_doc = docs_ref[block]
    present = jnp.int32(0)
    for distance in range(1, longest):
        source = block - distance
        same = (source >= 0) & (docs_ref[jnp.maximum(source, 0)] == own_doc)
        present = present + same.astype(jnp.int32)
    present_ref[...] = jnp.full(present_ref.shape, present, jnp.int32)


def earlier_kernel(head_count, longest, present_ref, *refs):
    packet_refs = refs[: longest - 1]
    turned_ref, peak_ref, total_ref, weighted_ref, out_ref, keys_ref, values_ref = refs[longest - 1 :]
    length = turned_ref.shape[0]
    head_size = turned_ref.shape[1] // head_count
    wide_size = length + head_size
    rate = math.log2(math.e) * head_size ** (-0.5)
    present = jnp.max(present_ref[...])
    odd = (lax.axis_index("inner") % 2) == 1
    steps = longest // 2 - 1
    apart_refs, swapped_refs, mixed_ref = (
        packet_refs[:steps],
        packet_refs[steps : 2 * steps],
        packet_refs[2 * steps],
    )
    slots = keys_ref.shape[0]

    def gather():
        transit = None
        for distance in range(1, longest):
            if distance % 2 == 0:
                packet = apart_refs[distance // 2 - 1][...]
            else:
                odd_ref = mixed_ref if distance == 1 else swapped_refs[(distance - 1) // 2 - 1]
                even_ref = (
                    mixed_ref if distance == longest - 1 else swapped_refs[(distance + 1) // 2 - 1]
                )
                packet = jnp.where(odd, odd_ref[...], even_ref[...])
            keys = packet[:, :length]
            own_transit = packet[:, length:wide_size]
            slot, place = (distance - 1) // GROUP, (distance - 1) % GROUP
            if distance == 1:
                transit = own_transit
            elif distance == 2:
                keys = dot(transit, keys).astype(BF16)
                transit = dot(transit, own_transit)
            else:
                high, low = halves(transit)
                keys = (dot(high, keys) + dot(low, keys)).astype(BF16)
                if distance < longest - 1:
                    transit = dot(high, own_transit) + dot(low, own_transit)
            keys_ref[slot, :, place * length : (place + 1) * length] = keys
            for part in range(length // head_size):
                start = wide_size + part * head_size
                row = place * length + part * head_size
                values_ref[slot, row : row + head_size, :head_size] = packet[
                    :, start : start + head_size
                ]
        for slot in range(slots):
            values_ref[slot, :, head_size:] = jnp.ones((GROUP * length, head_size), BF16)

    def visit(slot, blocks):
        keys = keys_ref[slot, :, : blocks * length]
        values = values_ref[slot, : blocks * length, :]
        for head in range(head_count):
            span = slice(head * head_size, (head + 1) * head_size)
            scores = dot(turned_ref[:, span], keys)
            old_peak = peak_ref[:, span]
            peak = row_peak(scores, old_peak)
            sums = dot(row_weights(scores, peak, rate), values)
            factor = jnp.exp2((old_peak - peak) * rate)
            total = total_ref[:, span] * factor + sums[:, head_size:]
            weighted = weighted_ref[:, span] * factor + sums[:, :head_size]
            if slots == 1:
                out_ref[:, span] = (weighted / total).astype(BF16)
            else:
                peak_ref[:, span] = peak
                total_ref[:, span] = total
                weighted_ref[:, span] = weighted

    def finish():
        for head in range(head_count):
            span = slice(head * head_size, (head + 1) * head_size)
            out_ref[:, span] = (weighted_ref[:, span] / total_ref[:, span]).astype(BF16)

    @pl.when(present > 0)
    def _():
        gather()

    if slots == 1:
        pl.when(present == 0)(finish)
        for blocks in range(1, longest):
            pl.when(present == blocks)(functools.partial(visit, 0, blocks))
    else:
        full = present // GROUP

        @pl.loop(0, full)
        def _(slot):
            visit(slot, GROUP)

        for blocks in range(1, GROUP):
            pl.when(present % GROUP == blocks)(functools.partial(visit, full, blocks))
        finish()


def vmem(count):
    return [pl.BlockSpec(memory_space=pltpu.VMEM)] * count


def in_hbm(value):
    return pltpu.with_memory_space_constraint(value, pltpu.HBM)


def permuted(value, target):
    count = lax.axis_size("outer") * lax.axis_size("inner")
    return lax.ppermute(value, AXES, [(i, target(i) % count) for i in range(count)])


def local(queries, keys, values, reflect, reflect_logit, doc_of_block):
    longest = lax.axis_size("outer") * lax.axis_size("inner") // 8
    length, head_size = keys.shape
    head_count = queries.shape[1] // head_size
    wide_size = length + head_size
    params = pltpu.CompilerParams(vmem_limit_bytes=VMEM_LIMIT)
    shape = jax.ShapeDtypeStruct
    hbm = pl.BlockSpec(memory_space=pltpu.HBM)
    packet, solved, gain, both, ones = pl.pallas_call(
        key_kernel,
        out_shape=(
            shape((head_size, wide_size + length), BF16),
            shape((length, 2 * wide_size), BF16),
            shape((8, length), F32),
            shape((head_size, 2 * length), BF16),
            shape((length, 2 * head_size), BF16),
        ),
        in_specs=[hbm] * 4,
        out_specs=tuple(vmem(5)),
        scratch_shapes=[
            pltpu.VMEM((length, head_size), BF16),
            pltpu.VMEM((length, head_size), BF16),
            pltpu.VMEM((1, length), F32),
            pltpu.SemaphoreType.DMA((4,)),
        ],
        compiler_params=params,
        cost_estimate=pl.CostEstimate(
            flops=40 * length**3, bytes_accessed=8 * length * length, transcendentals=length
        ),
        name="key_side",
    )(*(in_hbm(value) for value in (reflect, keys, values, reflect_logit.reshape(1, length))))
    apart = [permuted(packet, lambda i, s=s: i + 2 * s) for s in range(1, longest // 2)]
    mixed = permuted(packet, lambda i: i + longest - 1 if i % 2 else i + 1)
    wide = shape(queries.shape, F32)
    turned, peak, total, weighted, present = pl.pallas_call(
        functools.partial(query_kernel, head_count, longest),
        out_shape=(shape(queries.shape, BF16), wide, wide, wide, shape((8, 128), jnp.int32)),
        in_specs=[hbm] + vmem(5),
        out_specs=tuple(vmem(5)),
        scratch_shapes=[
            pltpu.SMEM(doc_of_block.shape, jnp.int32),
            pltpu.SemaphoreType.DMA(()),
        ],
        compiler_params=params,
        cost_estimate=pl.CostEstimate(
            flops=head_count * 10 * length**3,
            bytes_accessed=16 * length * length * head_count,
            transcendentals=head_count * length * length,
        ),
        name="query_side",
    )(in_hbm(doc_of_block), queries, both, ones, solved, gain)
    *apart, turned = lax.optimization_barrier((*apart, turned))
    swapped = [permuted(moved, lambda i: i ^ 1) for moved in apart]
    slots = (longest - 1 + GROUP - 1) // GROUP
    return pl.pallas_call(
        functools.partial(earlier_kernel, head_count, longest),
        out_shape=shape(queries.shape, BF16),
        in_specs=vmem(longest - 1 + 5),
        out_specs=vmem(1)[0],
        scratch_shapes=[
            pltpu.VMEM((slots, head_size, GROUP * length), BF16),
            pltpu.VMEM((slots, GROUP * length, 2 * head_size), BF16),
        ],
        compiler_params=params,
        cost_estimate=pl.CostEstimate(
            flops=head_count * 6 * length**3,
            bytes_accessed=16 * length * length * head_count,
            transcendentals=3 * head_count * length * length,
        ),
        name="earlier_blocks",
    )(present, *apart, *swapped, mixed, turned, peak, total, weighted)


def solution(mesh):
    placed = (
        P(AXES, None),
        P(AXES, None),
        P(AXES, None),
        P(AXES, None),
        P(AXES),
        P(),
    )
    return jax.shard_map(
        local, mesh=mesh, in_specs=placed, out_specs=P(AXES, None), check_vma=False
    )
```

time: 28.3 us -> 18.7 us (0.66); the launches traced: 28 us -> 19 us
  local copies, waits for them, and re-layouts: 3.85 us -> 0.01 us
  waiting for transfers between devices: 5.82 us -> 2.97 us
  Pallas kernels: 12 us -> 9.75 us
    unnamed x12 -> x2, local copies, waits for them, and re-layouts: 3.85 us -> 0.01 us
    pallas_call x1, Pallas kernels: 5.98 us -> 2.42 us  [local(): pl.pallas_call(functools.partial(earlier_kernel, head_count, longest), ou...]
    ppermute x3, waiting for transfers between devices: 5.82 us -> 2.97 us  [permuted(): lax.ppermute(value, AXES, [(i, target(i) % count) for i in range(count)])]
    pallas_call x2, Pallas kernels: 6.04 us -> 7.34 us  [the longest x1 3.88 us: local(): pl.pallas_call(functools.partial(query_kernel, head_count, longest), out_...]
  transfers between devices with their start and end apart: 3 -> 3, of which waited for: 1 -> 2; matrix products, arithmetic and copies ran while one was open for 0% -> 0% of each run, Pallas kernels for 13% -> 20%
where the time goes in v2:
time: 18.7 us; the launch traced here: 19 us
  Pallas kernels  9.75 us (52%)
  starting transfers between devices  6.23 us (33%)
  waiting for transfers between devices  2.97 us (16%)
    ppermute x3, starting transfers between devices, permuted(): lax.ppermute(value, AXES, [(i, target(i) % count) for i in range(count)])  6.23 us
    pallas_call x1, Pallas kernels, local(): pl.pallas_call(functools.partial(query_kernel, head_count, longest), out_...  3.88 us
    pallas_call x1, Pallas kernels, local(): pl.pallas_call(key_kernel, out_shape=(shape((head_size, wide_size + lengt...  3.46 us
    ppermute x3, waiting for transfers between devices, permuted(): lax.ppermute(value, AXES, [(i, target(i) % count) for i in range(count)])  2.97 us
    pallas_call x1, Pallas kernels, local(): pl.pallas_call(functools.partial(earlier_kernel, head_count, longest), ou...  2.42 us
  transfers between devices with their start and end apart: 3, of which 2 were waited for; matrix products, arithmetic and copies ran while one was open for 0% of the time, Pallas kernels for 20%

profile of v2, /device:TPU:1, one launch (start us, length us, event | category | flops | bytes accessed | tf_op | source)
XLA Modules:
  0.0 19.0 jit_solution(6138578864477841213)
XLA Ops:
  0.0 0.0 copy-start
  0.0 3.5 %key_side.1 = (bf16[128,640]{1,0:T(8,128)(2,1)S(1)}, bf16[256,768]{1,0:T(8,128)(2,1)S(1)}, f32[8,256]{1,0:T(8,128)S(1)}, bf16[128,512]{1,0:T(8,128)(2,1)S(1)}, bf16[256,256]{1,0:T(8,128)(2,1)S(1)}) custom-call(bf16[256,128]{1,0:T(8,128)(2,1)} %reflect_hbm.1, bf16[256,128]{1,0:T(8,128)(2,1)} %keys_hbm.1, bf16[256,128]{1,0:T(8,128)(2,1)} %values_hbm.1, ...), custom_call_target="tpu_custom_call" | custom-call | flops 671088640 | bytes 524288 | tf_op jit(solution)/shard_map/key_side/pallas_call | solution.py:325
  3.5 2.1 %collective-permute-start = (bf16[128,640]{1,0:T(8,128)(2,1)S(1)}, bf16[128,640]{1,0:T(8,128)(2,1)S(1)}, u32[]{:S(2)}, u32[]{:S(2)}) collective-permute-start(bf16[128,640]{1,0:T(8,128)(2,1)S(1)} %get-tuple-element.22), channel_id=1, source_target_pairs={{0,2},{1,3},{2,4},{3,5},{4,6},{5,7},{6,8},{7,9},{8,10},{9,11},{10,... | collective-permute-start | bytes 491528 | tf_op jit(solution)/shard_map/ppermute | solution.py:314
  5.6 2.1 %collective-permute-start.2 = (bf16[128,640]{1,0:T(8,128)(2,1)S(1)}, bf16[128,640]{1,0:T(8,128)(2,1)S(1)}, u32[]{:S(2)}, u32[]{:S(2)}) collective-permute-start(bf16[128,640]{1,0:T(8,128)(2,1)S(1)} %get-tuple-element.22), channel_id=1, source_target_pairs={{0,1},{1,4},{2,3},{3,6},{4,5},{5,8},{6,7},{7,10},{8,9},{9,12},{10,... | collective-permute-start | bytes 491528 | tf_op jit(solution)/shard_map/ppermute | solution.py:314
  7.6 0.0 copy-done
  7.6 3.9 %query_side.1 = (bf16[256,1024]{1,0:T(8,128)(2,1)S(1)}, f32[256,1024]{1,0:T(8,128)S(1)}, f32[256,1024]{1,0:T(8,128)S(1)}, f32[256,1024]{1,0:T(8,128)S(1)}, s32[8,128]{1,0:T(8,128)S(1)}) custom-call(s32[32]{0:T(128)} %docs_hbm.1, bf16[256,1024]{1,0:T(8,128)(2,1)S(1)} %copy-done, bf16[128,512]{1,0:T(8,128)(2,1)S(1)} %get-tuple-element.17.both_ref, ...), custom_call_target="tpu_custom_call" | custom-call | flops 1342177280 | bytes 8388608 | tf_op jit(solution)/shard_map/query_side/pallas_call | solution.py:351
  11.5 1.9 %collective-permute-done.refs_0_ = bf16[128,640]{1,0:T(8,128)(2,1)S(1)} collective-permute-done((bf16[128,640]{1,0:T(8,128)(2,1)S(1)}, bf16[128,640]{1,0:T(8,128)(2,1)S(1)}, u32[]{:S(2)}, u32[]{:S(2)}) %collective-permute-start) | collective-permute-done | bytes 163872 | tf_op jit(solution)/shard_map/ppermute | solution.py:314
  13.5 2.1 %collective-permute-start.1 = (bf16[128,640]{1,0:T(8,128)(2,1)S(1)}, bf16[128,640]{1,0:T(8,128)(2,1)S(1)}, u32[]{:S(2)}, u32[]{:S(2)}) collective-permute-start(bf16[128,640]{1,0:T(8,128)(2,1)S(1)} %collective-permute-done.refs_0_), channel_id=1, source_target_pairs={{0,1},{1,0},{2,3},{3,2},{4,5},{5,4},{6,7},{7,6},{8,9},{9,8},{10,11... | collective-permute-start | bytes 491528 | tf_op jit(solution)/shard_map/ppermute | solution.py:314
  15.5 0.0 collective-permute-done.2.refs_2_
  15.5 1.0 %collective-permute-done.1.refs_1_ = bf16[128,640]{1,0:T(8,128)(2,1)S(1)} collective-permute-done((bf16[128,640]{1,0:T(8,128)(2,1)S(1)}, bf16[128,640]{1,0:T(8,128)(2,1)S(1)}, u32[]{:S(2)}, u32[]{:S(2)}) %collective-permute-start.1) | collective-permute-done | bytes 163872 | tf_op jit(solution)/shard_map/ppermute | solution.py:314
  16.6 2.4 %earlier_blocks.1 = bf16[256,1024]{1,0:T(8,128)(2,1)} custom-call(s32[8,128]{1,0:T(8,128)S(1)} %get-tuple-element.21.present_ref, bf16[128,640]{1,0:T(8,128)(2,1)S(1)} %collective-permute-done.refs_0_, bf16[128,640]{1,0:T(8,128)(2,1)S(1)} %collective-permute-done.1.refs_1_, bf16[128,640]{1,0:T(8,128)(2,1)S(1)} %collective-permute-done.2.refs_2_, ...), custom_call_target="tpu_custom_call" | custom-call | flops 805306368 | bytes 8388608 | tf_op jit(solution)/shard_map/earlier_blocks/pallas_call | solution.py:371
Async XLA Ops:
  0.0 7.6 %copy-start = (bf16[256,1024]{1,0:T(8,128)(2,1)S(1)}, bf16[256,1024]{1,0:T(8,128)(2,1)}, u32[]{:S(2)}) copy-start(bf16[256,1024]{1,0:T(8,128)(2,1)} %queries_ref.1) | copy-start | bytes 1572868
  3.5 10.0 %collective-permute-start = (bf16[128,640]{1,0:T(8,128)(2,1)S(1)}, bf16[128,640]{1,0:T(8,128)(2,1)S(1)}, u32[]{:S(2)}, u32[]{:S(2)}) collective-permute-start(bf16[128,640]{1,0:T(8,128)(2,1)S(1)} %get-tuple-element.22), channel_id=1, source_target_pairs={{0,2},{1,3},{2,4},{3,5},{4,6},{5,7},{6,8},{7,9},{8,10},{9,11},{10,... | collective-permute-start | bytes 491528 | tf_op jit(solution)/shard_map/ppermute | solution.py:314
  5.6 10.0 %collective-permute-start.2 = (bf16[128,640]{1,0:T(8,128)(2,1)S(1)}, bf16[128,640]{1,0:T(8,128)(2,1)S(1)}, u32[]{:S(2)}, u32[]{:S(2)}) collective-permute-start(bf16[128,640]{1,0:T(8,128)(2,1)S(1)} %get-tuple-element.22), channel_id=1, source_target_pairs={{0,1},{1,4},{2,3},{3,6},{4,5},{5,8},{6,7},{7,10},{8,9},{9,12},{10,... | collective-permute-start | bytes 491528 | tf_op jit(solution)/shard_map/ppermute | solution.py:314
  13.5 3.1 %collective-permute-start.1 = (bf16[128,640]{1,0:T(8,128)(2,1)S(1)}, bf16[128,640]{1,0:T(8,128)(2,1)S(1)}, u32[]{:S(2)}, u32[]{:S(2)}) collective-permute-start(bf16[128,640]{1,0:T(8,128)(2,1)S(1)} %collective-permute-done.refs_0_), channel_id=1, source_target_pairs={{0,1},{1,0},{2,3},{3,2},{4,5},{5,4},{6,7},{7,6},{8,9},{9,8},{10,11... | collective-permute-start | bytes 491528 | tf_op jit(solution)/shard_map/ppermute | solution.py:314

commit v3 on v2

--- a/solution.py
+++ b/solution.py
@@ -12,7 +12,7 @@
 BF16 = jnp.bfloat16
 AXES = ("outer", "inner")
 GROUP = 3
-VMEM_LIMIT = 48 * 1024 * 1024
+VMEM_LIMIT = 24 * 1024 * 1024
 
 
 def dot(left, right):
@@ -137,39 +137,31 @@
         ]
 
 
+def lane_pieces(scores, size):
+    return [score[:, i : i + size] for score in scores for i in range(0, score.shape[1], size)]
+
+
 def row_peak(scores, peak):
-    size = peak.shape[1]
-    pieces = [scores[:, i : i + size] for i in range(0, scores.shape[1], size)]
-    return jnp.maximum(peak, jnp.max(functools.reduce(jnp.maximum, pieces), axis=1, keepdims=True))
+    largest = functools.reduce(jnp.maximum, lane_pieces(scores, peak.shape[1]))
+    return jnp.maximum(peak, jnp.max(largest, axis=1, keepdims=True))
 
 
 def row_weights(scores, peak, rate):
-    size = peak.shape[1]
-    pieces = [
-        jnp.exp2((scores[:, i : i + size] - peak) * rate) for i in range(0, scores.shape[1], size)
-    ]
+    pieces = [jnp.exp2((piece - peak) * rate) for piece in lane_pieces(scores, peak.shape[1])]
     return jnp.concatenate(pieces, axis=1).astype(BF16)
 
 
-def query_kernel(
-    head_count,
-    longest,
-    docs_hbm,
-    queries_ref,
-    both_ref,
-    ones_ref,
-    solved_ref,
-    gain_ref,
-    turned_ref,
-    peak_ref,
-    total_ref,
-    weighted_ref,
-    present_ref,
-    docs_ref,
-    docs_sem,
-):
-    docs_copy = pltpu.make_async_copy(docs_hbm, docs_ref, docs_sem)
-    docs_copy.start()
+def reciprocal(value):
+    rough = pl.reciprocal(value, approx=True)
+    return rough * (2.0 - value * rough)
+
+
+def query_kernel(heads, longest, *refs):
+    docs_hbm, queries_ref, both_ref, ones_ref, solved_ref, gain_ref = refs[:6]
+    turned_ref, peak_ref, total_ref, weighted_ref, present_ref, docs_ref, docs_sem = refs[-7:]
+    if docs_hbm is not None:
+        docs_copy = pltpu.make_async_copy(docs_hbm, docs_ref, docs_sem)
+        docs_copy.start()
     length = ones_ref.shape[0]
     head_size = ones_ref.shape[1] // 2
     wide_size = length + head_size
@@ -183,7 +175,7 @@
     solved_high = solved_ref[:, :wide_size]
     solved_low = solved_ref[:, wide_size:]
     values = ones_ref[...]
-    for head in range(head_count):
+    for head in heads:
         span = slice(head * head_size, (head + 1) * head_size)
         queries = queries_ref[:, span]
         faced = dot(queries, both)
@@ -191,105 +183,188 @@
         scores = (faced[:, length:] - change[:, :length]) + hidden
         turned_ref[:, span] = (queries.astype(F32) - change[:, length:]).astype(BF16)
         peak = jnp.broadcast_to(jnp.max(scores, axis=1, keepdims=True), (length, head_size))
-        sums = dot(row_weights(scores, peak, rate), values)
+        sums = dot(row_weights([scores], peak, rate), values)
         peak_ref[:, span] = peak
         weighted_ref[:, span] = sums[:, :head_size]
         total_ref[:, span] = sums[:, head_size:]
-    docs_copy.wait()
-    block = lax.axis_index("outer") * lax.axis_size("inner") + lax.axis_index("inner")
-    own_doc = docs_ref[block]
-    present = jnp.int32(0)
-    for distance in range(1, longest):
-        source = block - distance
-        same = (source >= 0) & (docs_ref[jnp.maximum(source, 0)] == own_doc)
-        present = present + same.astype(jnp.int32)
-    present_ref[...] = jnp.full(present_ref.shape, present, jnp.int32)
+    if docs_hbm is not None:
+        docs_copy.wait()
+        block = lax.axis_index("outer") * lax.axis_size("inner") + lax.axis_index("inner")
+        own_doc = docs_ref[block]
+        present = jnp.int32(0)
+        for distance in range(1, longest):
+            source = block - distance
+            same = (source >= 0) & (docs_ref[jnp.maximum(source, 0)] == own_doc)
+            present = present + same.astype(jnp.int32)
+        present_ref[...] = jnp.full(present_ref.shape, present, jnp.int32)
+
+
+def other_queries(heads, longest, *refs):
+    for done_ref, state_ref in zip(refs[5:9], refs[9:13]):
+        state_ref[:, : done_ref.shape[1]] = done_ref[...]
+    query_kernel(heads, longest, None, *refs, None, None, None)
+
+
+def is_odd():
+    return (lax.axis_index("inner") % 2) == 1
+
+
+def put_out(out_ref, out_hbm, out_sems, head, head_size):
+    span = slice(head * head_size, (head + 1) * head_size)
+    return pltpu.make_async_copy(out_ref.at[:, span], out_hbm.at[:, span], out_sems.at[head])
+
+
+def attend(head_count, state_refs, new_refs, all_keys, values, out_refs):
+    turned_ref, peak_ref, total_ref, weighted_ref = state_refs
+    head_size = turned_ref.shape[1] // head_count
+    rate = math.log2(math.e) * head_size ** (-0.5)
+    for head in range(head_count):
+        span = slice(head * head_size, (head + 1) * head_size)
+        old_peak = peak_ref[:, span]
+        scores = [dot(turned_ref[:, span], keys) for keys in all_keys]
+        peak = row_peak(scores, old_peak)
+        sums = dot(row_weights(scores, peak, rate), values)
+        factor = jnp.exp2((old_peak - peak) * rate)
+        total = total_ref[:, span] * factor + sums[:, head_size:]
+        weighted = weighted_ref[:, span] * factor + sums[:, :head_size]
+        if out_refs is not None:
+            out_refs[0][:, span] = (weighted * reciprocal(total)).astype(BF16)
+            put_out(*out_refs, head, head_size).start()
+        else:
+            for new_ref, new in zip(new_refs, (peak, total, weighted)):
+                new_ref[:, span] = new
+    if out_refs is not None:
+        wait_out(head_count, out_refs)
+
+
+def finish(head_count, sum_refs, out_refs):
+    total_ref, weighted_ref = sum_refs
+    head_size = total_ref.shape[1] // head_count
+    for head in range(head_count):
+        span = slice(head * head_size, (head + 1) * head_size)
+        out_refs[0][:, span] = (weighted_ref[:, span] * reciprocal(total_ref[:, span])).astype(BF16)
+        put_out(*out_refs, head, head_size).start()
+    wait_out(head_count, out_refs)
+
+
+def wait_out(head_count, out_refs):
+    head_size = out_refs[0].shape[1] // head_count
+    for head in range(head_count):
+        put_out(*out_refs, head, head_size).wait()
+
+
+def store_values(values_ref, slot, place, packet, length):
+    head_size = packet.shape[0]
+    rows = pl.ds(place * length, length)
+    start = length + head_size
+    pieces = [
+        packet[:, at : at + head_size] for at in range(start, start + length, head_size)
+    ]
+    values_ref[slot, rows, :head_size] = jnp.concatenate(pieces, axis=0)
+    values_ref[slot, rows, head_size:] = jnp.ones((length, head_size), BF16)
+
+
+def nearest_kernel(head_count, present_ref, mixed_ref, *refs):
+    old_refs, new_refs = refs[:4], refs[4:7]
+    out_hbm, out_ref, values_ref, out_sems = refs[7:]
+    out_refs = (out_ref, out_hbm, out_sems)
+    length = out_ref.shape[0]
+    present = jnp.max(present_ref[...])
+    odd = is_odd()
+
+    def nearest(out):
+        packet = mixed_ref[...]
+        store_values(values_ref, 0, 0, packet, length)
+        attend(head_count, old_refs, new_refs, [packet[:, :length]], values_ref[0], out)
+
+    @pl.when(present == 0)
+    def _():
+        finish(head_count, old_refs[2:], out_refs)
+
+    pl.when(odd & (present == 1))(lambda: nearest(out_refs))
+    pl.when(odd & (present > 1))(lambda: nearest(None))
+
+    @pl.when(jnp.logical_not(odd) & (present > 0))
+    def _():
+        for old_ref, new_ref in zip(old_refs[1:], new_refs):
+            new_ref[...] = old_ref[...]
 
 
 def earlier_kernel(head_count, longest, present_ref, *refs):
     packet_refs = refs[: longest - 1]
-    turned_ref, peak_ref, total_ref, weighted_ref, out_ref, keys_ref, values_ref = refs[longest - 1 :]
-    length = turned_ref.shape[0]
-    head_size = turned_ref.shape[1] // head_count
+    state_refs = refs[longest - 1 : longest + 3]
+    out_hbm, out_ref, keys_ref, values_ref, out_sems = refs[-5:]
+    out_refs = (out_ref, out_hbm, out_sems)
+    present = jnp.max(present_ref[...])
+    length = out_ref.shape[0]
+    head_size = out_ref.shape[1] // head_count
     wide_size = length + head_size
-    rate = math.log2(math.e) * head_size ** (-0.5)
-    present = jnp.max(present_ref[...])
-    odd = (lax.axis_index("inner") % 2) == 1
+    odd = is_odd()
     steps = longest // 2 - 1
     apart_refs, swapped_refs, mixed_ref = (
         packet_refs[:steps],
         packet_refs[steps : 2 * steps],
         packet_refs[2 * steps],
     )
-    slots = keys_ref.shape[0]
-
-    def gather():
+    slots = values_ref.shape[0]
+
+    def packet_of(distance, known_odd):
+        if distance % 2 == 0:
+            return apart_refs[distance // 2 - 1][...]
+        odd_ref = mixed_ref if distance == 1 else swapped_refs[(distance - 1) // 2 - 1]
+        even_ref = mixed_ref if distance == longest - 1 else swapped_refs[(distance + 1) // 2 - 1]
+        if known_odd is None:
+            return jnp.where(odd, odd_ref[...], even_ref[...])
+        return (odd_ref if known_odd else even_ref)[...]
+
+    def collect(first, last, known_odd=None):
         transit = None
-        for distance in range(1, longest):
-            if distance % 2 == 0:
-                packet = apart_refs[distance // 2 - 1][...]
-            else:
-                odd_ref = mixed_ref if distance == 1 else swapped_refs[(distance - 1) // 2 - 1]
-                even_ref = (
-                    mixed_ref if distance == longest - 1 else swapped_refs[(distance + 1) // 2 - 1]
-                )
-                packet = jnp.where(odd, odd_ref[...], even_ref[...])
+        all_keys = []
+        for distance in range(1, last + 1):
+            packet = packet_of(distance, known_odd)
             keys = packet[:, :length]
             own_transit = packet[:, length:wide_size]
-            slot, place = (distance - 1) // GROUP, (distance - 1) % GROUP
             if distance == 1:
                 transit = own_transit
             elif distance == 2:
                 keys = dot(transit, keys).astype(BF16)
-                transit = dot(transit, own_transit)
+                if distance < last:
+                    transit = dot(transit, own_transit)
             else:
                 high, low = halves(transit)
                 keys = (dot(high, keys) + dot(low, keys)).astype(BF16)
-                if distance < longest - 1:
+                if distance < last:
                     transit = dot(high, own_transit) + dot(low, own_transit)
-            keys_ref[slot, :, place * length : (place + 1) * length] = keys
-            for part in range(length // head_size):
-                start = wide_size + part * head_size
-                row = place * length + part * head_size
-                values_ref[slot, row : row + head_size, :head_size] = packet[
-                    :, start : start + head_size
-                ]
-        for slot in range(slots):
-            values_ref[slot, :, head_size:] = jnp.ones((GROUP * length, head_size), BF16)
-
-    def visit(slot, blocks):
-        keys = keys_ref[slot, :, : blocks * length]
-        values = values_ref[slot, : blocks * length, :]
-        for head in range(head_count):
-            span = slice(head * head_size, (head + 1) * head_size)
-            scores = dot(turned_ref[:, span], keys)
-            old_peak = peak_ref[:, span]
-            peak = row_peak(scores, old_peak)
-            sums = dot(row_weights(scores, peak, rate), values)
-            factor = jnp.exp2((old_peak - peak) * rate)
-            total = total_ref[:, span] * factor + sums[:, head_size:]
-            weighted = weighted_ref[:, span] * factor + sums[:, :head_size]
-            if slots == 1:
-                out_ref[:, span] = (weighted / total).astype(BF16)
-            else:
-                peak_ref[:, span] = peak
-                total_ref[:, span] = total
-                weighted_ref[:, span] = weighted
-
-    def finish():
-        for head in range(head_count):
-            span = slice(head * head_size, (head + 1) * head_size)
-            out_ref[:, span] = (weighted_ref[:, span] / total_ref[:, span]).astype(BF16)
-
-    @pl.when(present > 0)
-    def _():
-        gather()
+            if distance >= first:
+                all_keys.append(keys)
+                index = distance - first
+                store_values(values_ref, index // GROUP, index % GROUP, packet, length)
+        return all_keys
 
     if slots == 1:
-        pl.when(present == 0)(finish)
-        for blocks in range(1, longest):
-            pl.when(present == blocks)(functools.partial(visit, 0, blocks))
+        for known_odd in (False, True):
+            first = 2 if known_odd else 1
+            for last in range(first, longest):
+
+                @pl.when((odd == known_odd) & (present == last))
+                def _(known_odd=known_odd, first=first, last=last):
+                    keys = collect(first, last, known_odd)
+                    values = values_ref[0, : len(keys) * length, :]
+                    attend(head_count, state_refs, None, keys, values, out_refs)
+
     else:
+
+        @pl.when(present > 0)
+        def _():
+            for index, keys in enumerate(collect(1, longest - 1)):
+                slot, place = index // GROUP, index % GROUP
+                keys_ref[slot, :, place * length : (place + 1) * length] = keys
+
+        def visit(slot, blocks):
+            keys = [keys_ref[slot, :, i * length : (i + 1) * length] for i in range(blocks)]
+            values = values_ref[slot, : blocks * length, :]
+            attend(head_count, state_refs, state_refs[1:], keys, values, None)
+
         full = present // GROUP
 
         @pl.loop(0, full)
@@ -298,7 +373,7 @@
 
         for blocks in range(1, GROUP):
             pl.when(present % GROUP == blocks)(functools.partial(visit, full, blocks))
-        finish()
+        finish(head_count, state_refs[2:], out_refs)
 
 
 def vmem(count):
@@ -346,11 +421,21 @@
         name="key_side",
     )(*(in_hbm(value) for value in (reflect, keys, values, reflect_logit.reshape(1, length))))
     apart = [permuted(packet, lambda i, s=s: i + 2 * s) for s in range(1, longest // 2)]
-    mixed = permuted(packet, lambda i: i + longest - 1 if i % 2 else i + 1)
     wide = shape(queries.shape, F32)
-    turned, peak, total, weighted, present = pl.pallas_call(
-        functools.partial(query_kernel, head_count, longest),
-        out_shape=(shape(queries.shape, BF16), wide, wide, wide, shape((8, 128), jnp.int32)),
+    state_shapes = (shape(queries.shape, BF16), wide, wide, wide)
+    first = max(1, head_count // 4)
+    first_shapes = [shape((length, first * head_size), part.dtype) for part in state_shapes]
+
+    def query_cost(heads):
+        return pl.CostEstimate(
+            flops=heads * 10 * length**3,
+            bytes_accessed=16 * length * length * heads,
+            transcendentals=heads * length * length,
+        )
+
+    *state, present = pl.pallas_call(
+        functools.partial(query_kernel, range(first), longest),
+        out_shape=(*first_shapes, shape((8, 128), jnp.int32)),
         in_specs=[hbm] + vmem(5),
         out_specs=tuple(vmem(5)),
         scratch_shapes=[
@@ -358,24 +443,58 @@
             pltpu.SemaphoreType.DMA(()),
         ],
         compiler_params=params,
-        cost_estimate=pl.CostEstimate(
-            flops=head_count * 10 * length**3,
-            bytes_accessed=16 * length * length * head_count,
-            transcendentals=head_count * length * length,
-        ),
-        name="query_side",
+        cost_estimate=query_cost(first),
+        name="first_queries",
     )(in_hbm(doc_of_block), queries, both, ones, solved, gain)
-    *apart, turned = lax.optimization_barrier((*apart, turned))
+    mixed_packet, state[0] = lax.optimization_barrier((packet, state[0]))
+    mixed = permuted(mixed_packet, lambda i: i + longest - 1 if i % 2 else i + 1)
+    state = pl.pallas_call(
+        functools.partial(other_queries, range(first, head_count), longest),
+        out_shape=state_shapes,
+        in_specs=vmem(9),
+        out_specs=tuple(vmem(4)),
+        compiler_params=params,
+        cost_estimate=query_cost(head_count - first),
+        name="other_queries",
+    )(queries, both, ones, solved, gain, *state)
+    *apart, turned = lax.optimization_barrier((*apart, state[0]))
+    state = [turned, *state[1:]]
     swapped = [permuted(moved, lambda i: i ^ 1) for moved in apart]
+    out_shape = shape(queries.shape, BF16)
     slots = (longest - 1 + GROUP - 1) // GROUP
+    out_scratch = [pltpu.VMEM(queries.shape, BF16), pltpu.SemaphoreType.DMA((head_count,))]
+    sums, started = state[1:], []
+    if slots == 1:
+        *sums, out = pl.pallas_call(
+            functools.partial(nearest_kernel, head_count),
+            out_shape=(*state_shapes[1:], out_shape),
+            in_specs=vmem(6),
+            out_specs=(*vmem(3), hbm),
+            scratch_shapes=[
+                out_scratch[0],
+                pltpu.VMEM((1, length, 2 * head_size), BF16),
+                out_scratch[1],
+            ],
+            compiler_params=params,
+            cost_estimate=pl.CostEstimate(
+                flops=head_count * 2 * length**3,
+                bytes_accessed=4 * length * length * head_count,
+                transcendentals=head_count * length * length,
+            ),
+            name="nearest_block",
+        )(present, mixed, *state)
+        started = [in_hbm(out)]
     return pl.pallas_call(
         functools.partial(earlier_kernel, head_count, longest),
-        out_shape=shape(queries.shape, BF16),
-        in_specs=vmem(longest - 1 + 5),
-        out_specs=vmem(1)[0],
+        out_shape=out_shape,
+        in_specs=vmem(longest - 1 + 5) + [hbm] * len(started),
+        out_specs=hbm,
+        input_output_aliases={longest + 4: 0} if started else {},
         scratch_shapes=[
+            out_scratch[0],
             pltpu.VMEM((slots, head_size, GROUP * length), BF16),
             pltpu.VMEM((slots, GROUP * length, 2 * head_size), BF16),
+            out_scratch[1],
         ],
         compiler_params=params,
         cost_estimate=pl.CostEstimate(
@@ -384,7 +503,7 @@
             transcendentals=3 * head_count * length * length,
         ),
         name="earlier_blocks",
-    )(present, *apart, *swapped, mixed, turned, peak, total, weighted)
+    )(present, *apart, *swapped, mixed, turned, *sums, *started)
 
 
 def solution(mesh):

time: 18.7 us -> 17.6 us (0.941)
  waiting for transfers between devices: 2.97 us -> 1.89 us
  starting transfers between devices: 6.23 us -> 5.83 us
  Pallas kernels: 9.75 us -> 9.95 us
    pallas_call x1 -> x3, Pallas kernels: 3.88 us -> 6.01 us  [the longest x1 2.79 us: local(): pl.pallas_call(functools.partial(other_queries, range(first, head_count),...]
    pallas_call x1, Pallas kernels: 2.42 us -> 0.48 us  [local(): pl.pallas_call(functools.partial(earlier_kernel, head_count, longest), ou...]
    ppermute x3, waiting for transfers between devices: 2.97 us -> 1.89 us  [permuted(): lax.ppermute(value, AXES, [(i, target(i) % count) for i in range(count)])]
    ppermute x3, starting transfers between devices: 6.23 us -> 5.83 us  [permuted(): lax.ppermute(value, AXES, [(i, target(i) % count) for i in range(count)])]
  transfers between devices with their start and end apart: 3 -> 3, of which waited for: 2 -> 1; matrix products, arithmetic and copies ran while one was open for 0% -> 0% of each run, Pallas kernels for 20% -> 34%
where the time goes in v3:
time: 17.6 us; the launch traced here: 17.9 us
  Pallas kernels  9.95 us (57%)
  starting transfers between devices  5.83 us (33%)
  waiting for transfers between devices  1.89 us (11%)
  between operations  0.2 us (1%)
    ppermute x3, starting transfers between devices, permuted(): lax.ppermute(value, AXES, [(i, target(i) % count) for i in range(count)])  5.83 us
    pallas_call x1, Pallas kernels, local(): pl.pallas_call(key_kernel, out_shape=(shape((head_size, wide_size + lengt...  3.46 us
    pallas_call x1, Pallas kernels, local(): pl.pallas_call(functools.partial(other_queries, range(first, head_count),...  2.79 us
    pallas_call x1, Pallas kernels, local(): pl.pallas_call(functools.partial(nearest_kernel, head_count), out_shape=(...  2.12 us
    ppermute x3, waiting for transfers between devices, permuted(): lax.ppermute(value, AXES, [(i, target(i) % count) for i in range(count)])  1.89 us
    pallas_call x1, Pallas kernels, local(): pl.pallas_call(functools.partial(query_kernel, range(first), longest), ou...  1.1 us
    pallas_call x1, Pallas kernels, local(): pl.pallas_call(functools.partial(earlier_kernel, head_count, longest), ou...  0.48 us
  transfers between devices with their start and end apart: 3, of which 1 were waited for; matrix products, arithmetic and copies ran while one was open for 0% of the time, Pallas kernels for 34%

profile of v3, /device:TPU:1, one launch (start us, length us, event | category | flops | bytes accessed | tf_op | source)
XLA Modules:
  0.0 17.9 jit_solution(6379844975995344566)
XLA Ops:
  0.0 0.0 copy-start
  0.0 3.5 %key_side.1 = (bf16[128,640]{1,0:T(8,128)(2,1)S(1)}, bf16[256,768]{1,0:T(8,128)(2,1)S(1)}, f32[8,256]{1,0:T(8,128)S(1)}, bf16[128,512]{1,0:T(8,128)(2,1)S(1)}, bf16[256,256]{1,0:T(8,128)(2,1)S(1)}) custom-call(bf16[256,128]{1,0:T(8,128)(2,1)} %reflect_hbm.1, bf16[256,128]{1,0:T(8,128)(2,1)} %keys_hbm.1, bf16[256,128]{1,0:T(8,128)(2,1)} %values_hbm.1, ...), custom_call_target="tpu_custom_call" | custom-call | flops 671088640 | bytes 524288 | tf_op jit(solution)/shard_map/key_side/pallas_call | solution.py:400
  3.5 2.1 %collective-permute-start = (bf16[128,640]{1,0:T(8,128)(2,1)S(1)}, bf16[128,640]{1,0:T(8,128)(2,1)S(1)}, u32[]{:S(2)}, u32[]{:S(2)}) collective-permute-start(bf16[128,640]{1,0:T(8,128)(2,1)S(1)} %get-tuple-element.40), channel_id=1, source_target_pairs={{0,2},{1,3},{2,4},{3,5},{4,6},{5,7},{6,8},{7,9},{8,10},{9,11},{10,... | collective-permute-start | bytes 491528 | tf_op jit(solution)/shard_map/ppermute | solution.py:389
  5.6 0.0 copy-done
  5.6 1.1 %first_queries.1 = (bf16[256,256]{1,0:T(8,128)(2,1)S(1)}, f32[256,256]{1,0:T(8,128)S(1)}, f32[256,256]{1,0:T(8,128)S(1)}, f32[256,256]{1,0:T(8,128)S(1)}, s32[8,128]{1,0:T(8,128)S(1)}) custom-call(s32[32]{0:T(128)} %refs_0_.2, bf16[256,1024]{1,0:T(8,128)(2,1)S(1)} %copy-done, bf16[128,512]{1,0:T(8,128)(2,1)S(1)} %get-tuple-element.27.refs_2_.refs_1_, ...), custom_call_target="tpu_custom_call" | custom-call | flops 335544320 | bytes 2097152 | tf_op jit(solution)/shard_map/first_queries/pallas_call | solution.py:436
  6.7 2.1 %collective-permute-start.2 = (bf16[128,640]{1,0:T(8,128)(2,1)S(1)}, bf16[128,640]{1,0:T(8,128)(2,1)S(1)}, u32[]{:S(2)}, u32[]{:S(2)}) collective-permute-start(bf16[128,640]{1,0:T(8,128)(2,1)S(1)} %get-tuple-element.40), channel_id=1, source_target_pairs={{0,1},{1,4},{2,3},{3,6},{4,5},{5,8},{6,7},{7,10},{8,9},{9,12},{10,... | collective-permute-start | bytes 491528 | tf_op jit(solution)/shard_map/ppermute | solution.py:389
  8.8 2.8 %other_queries.1 = (bf16[256,1024]{1,0:T(8,128)(2,1)S(1)}, f32[256,1024]{1,0:T(8,128)S(1)}, f32[256,1024]{1,0:T(8,128)S(1)}, f32[256,1024]{1,0:T(8,128)S(1)}) custom-call(bf16[256,1024]{1,0:T(8,128)(2,1)S(1)} %copy-done, bf16[128,512]{1,0:T(8,128)(2,1)S(1)} %get-tuple-element.27.refs_2_.refs_1_, bf16[256,256]{1,0:T(8,128)(2,1)S(1)} %get-tuple-element.28.refs_3_.refs_2_, ...), custom_call_target="tpu_custom_call" | custom-call | flops 1006632960 | bytes 6291456 | tf_op jit(solution)/shard_map/other_queries/pallas_call | solution.py:451
  11.6 1.9 %collective-permute-done.refs_0_ = bf16[128,640]{1,0:T(8,128)(2,1)S(1)} collective-permute-done((bf16[128,640]{1,0:T(8,128)(2,1)S(1)}, bf16[128,640]{1,0:T(8,128)(2,1)S(1)}, u32[]{:S(2)}, u32[]{:S(2)}) %collective-permute-start) | collective-permute-done | bytes 163872 | tf_op jit(solution)/shard_map/ppermute | solution.py:389
  13.5 1.6 %collective-permute-start.1 = (bf16[128,640]{1,0:T(8,128)(2,1)S(1)}, bf16[128,640]{1,0:T(8,128)(2,1)S(1)}, u32[]{:S(2)}, u32[]{:S(2)}) collective-permute-start(bf16[128,640]{1,0:T(8,128)(2,1)S(1)} %collective-permute-done.refs_0_), channel_id=1, source_target_pairs={{0,1},{1,0},{2,3},{3,2},{4,5},{5,4},{6,7},{7,6},{8,9},{9,8},{10,11... | collective-permute-start | bytes 491528 | tf_op jit(solution)/shard_map/ppermute | solution.py:389
  15.1 0.0 collective-permute-done.2.mixed_ref.refs_2_
  15.1 2.1 %nearest_block.1 = (f32[256,1024]{1,0:T(8,128)S(1)}, f32[256,1024]{1,0:T(8,128)S(1)}, f32[256,1024]{1,0:T(8,128)S(1)}, bf16[256,1024]{1,0:T(8,128)(2,1)}) custom-call(s32[8,128]{1,0:T(8,128)S(1)} %get-tuple-element.31.present_ref, bf16[128,640]{1,0:T(8,128)(2,1)S(1)} %collective-permute-done.2.mixed_ref.refs_2_, ...), custom_call_target="tpu_custom_call" | custom-call | flops 268435456 | bytes 2097152 | tf_op jit(solution)/shard_map/nearest_block/pallas_call | solution.py:468
  17.2 0.0 collective-permute-done.1.refs_1_
  17.2 0.5 %earlier_blocks.1 = bf16[256,1024]{1,0:T(8,128)(2,1)} custom-call(s32[8,128]{1,0:T(8,128)S(1)} %get-tuple-element.31.present_ref, bf16[128,640]{1,0:T(8,128)(2,1)S(1)} %collective-permute-done.refs_0_, bf16[128,640]{1,0:T(8,128)(2,1)S(1)} %collective-permute-done.1.refs_1_, ...), custom_call_target="tpu_custom_call", output_to_operand_aliasing={{}: (8, {})} | custom-call | flops 805306368 | bytes 8388608 | tf_op jit(solution)/shard_map/earlier_blocks/pallas_call | solution.py:487
Async XLA Ops:
  0.0 5.6 %copy-start = (bf16[256,1024]{1,0:T(8,128)(2,1)S(1)}, bf16[256,1024]{1,0:T(8,128)(2,1)}, u32[]{:S(2)}) copy-start(bf16[256,1024]{1,0:T(8,128)(2,1)} %refs_0_.3) | copy-start | bytes 1572868
  3.5 10.0 %collective-permute-start = (bf16[128,640]{1,0:T(8,128)(2,1)S(1)}, bf16[128,640]{1,0:T(8,128)(2,1)S(1)}, u32[]{:S(2)}, u32[]{:S(2)}) collective-permute-start(bf16[128,640]{1,0:T(8,128)(2,1)S(1)} %get-tuple-element.40), channel_id=1, source_target_pairs={{0,2},{1,3},{2,4},{3,5},{4,6},{5,7},{6,8},{7,9},{8,10},{9,11},{10,... | collective-permute-start | bytes 491528 | tf_op jit(solution)/shard_map/ppermute | solution.py:389
  6.7 8.4 %collective-permute-start.2 = (bf16[128,640]{1,0:T(8,128)(2,1)S(1)}, bf16[128,640]{1,0:T(8,128)(2,1)S(1)}, u32[]{:S(2)}, u32[]{:S(2)}) collective-permute-start(bf16[128,640]{1,0:T(8,128)(2,1)S(1)} %get-tuple-element.40), channel_id=1, source_target_pairs={{0,1},{1,4},{2,3},{3,6},{4,5},{5,8},{6,7},{7,10},{8,9},{9,12},{10,... | collective-permute-start | bytes 491528 | tf_op jit(solution)/shard_map/ppermute | solution.py:389
  13.5 3.7 %collective-permute-start.1 = (bf16[128,640]{1,0:T(8,128)(2,1)S(1)}, bf16[128,640]{1,0:T(8,128)(2,1)S(1)}, u32[]{:S(2)}, u32[]{:S(2)}) collective-permute-start(bf16[128,640]{1,0:T(8,128)(2,1)S(1)} %collective-permute-done.refs_0_), channel_id=1, source_target_pairs={{0,1},{1,0},{2,3},{3,2},{4,5},{5,4},{6,7},{7,6},{8,9},{9,8},{10,11... | collective-permute-start | bytes 491528 | tf_op jit(solution)/shard_map/ppermute | solution.py:389

commit v4 on v3

--- a/solution.py
+++ b/solution.py
@@ -40,14 +40,20 @@
     identity = (rows == columns).astype(F32)
     results = [identity - part for part in strict_parts]
     powers = [halves(part) for part in strict_parts]
-    reach = 2
+    powers = [dot_halves(power, power) for power in powers]
+    reach = 4
     while reach < length:
-        powers = [halves(dot_halves(power, power)) for power in powers]
-        results = [
-            result + dot_halves(halves(result), power) for result, power in zip(results, powers)
-        ]
+        for index, (result, power) in enumerate(zip(results, powers)):
+            high, low = halves(jnp.concatenate([power, result], axis=0))
+            weights = (high[:length], low[:length])
+            product = dot_halves((high, low), weights)
+            powers[index] = product[:length]
+            results[index] = result + product[length:]
         reach = reach * 2
-    return results
+    return [
+        result + dot_halves(halves(result), halves(power))
+        for result, power in zip(results, powers)
+    ]
 
 
 def key_kernel(
@@ -56,7 +62,7 @@
     values_hbm,
     logit_hbm,
     packet_ref,
-    solved_ref,
+    partial_ref,
     gain_ref,
     turned_ref,
     ones_ref,
@@ -98,36 +104,32 @@
     keys_turned = keys.astype(F32).T
     turned_ref[:, :length] = reflect_turned.astype(BF16)
     turned_ref[:, length:] = keys_turned.astype(BF16)
-    scaled = halves(reflect_turned * gain)
+    scaled_high, scaled_low = halves(reflect_turned * gain)
+    scaled_first = (scaled_high[:, :half], scaled_low[:, :half])
+    scaled_second = (scaled_high[:, half:], scaled_low[:, half:])
+    across = halves(chained[half:, :half])
+    wide = halves(jnp.concatenate([facing[:half, :half], reflect_float[:half]], axis=1))
+    tall = halves(
+        jnp.concatenate([facing[half:, :half], reflect_float[half:], facing[half:, half:]], axis=1)
+    )
     first, second = unit_inverses([chained[:half, :half], chained[half:, half:]])
-    first, second = halves(first), halves(second)
-    wide = jnp.concatenate([facing[:half, :half], reflect_float[:half]], axis=1)
-    upper = dot_halves(first, halves(wide))
-    tall = jnp.concatenate([facing[half:, :half], reflect_float[half:], facing[half:, half:]], axis=1)
-    lower = dot_halves(second, halves(tall))
-    bridge = dot_halves(second, halves(chained[half:, :half]))
-    cross = dot_halves(halves(bridge), halves(upper))
-    lower_left = lower[:, : half + head_size] - cross
-    solved = jnp.concatenate(
-        [
-            jnp.concatenate(
-                [upper[:, :half], jnp.zeros((half, half), F32), upper[:, half:]], axis=1
-            ),
-            jnp.concatenate(
-                [lower_left[:, :half], lower[:, half + head_size :], lower_left[:, half:]], axis=1
-            ),
-        ],
-        axis=0,
-    )
-    solved = halves(solved)
-    solved_ref[:, :wide_size] = solved[0]
-    solved_ref[:, wide_size:] = solved[1]
-    change = dot_halves(scaled, solved)
+    upper = dot_halves(halves(first), wide)
+    reach = halves(dot_halves(scaled_second, halves(second)))
+    bridge = dot_halves(reach, across)
+    upper_halves = halves(upper)
+    own = dot_halves(scaled_first, upper_halves)
+    later = dot_halves(reach, tall)
+    change = (own + later[:, :wide_size - half]) - dot_halves(halves(bridge), upper_halves)
+    partial_ref[:, :half] = second
+    partial_ref[:, half:length] = chained[half:, :half]
+    partial_ref[:, length : 2 * length] = facing[half:, :]
+    partial_ref[:, 2 * length :] = upper
     head_rows = lax.broadcasted_iota(jnp.int32, (head_size, head_size), 0)
     head_columns = lax.broadcasted_iota(jnp.int32, (head_size, head_size), 1)
     identity = (head_rows == head_columns).astype(F32)
-    packet_ref[:, :length] = (keys_turned - change[:, :length]).astype(BF16)
-    packet_ref[:, length:wide_size] = (identity - change[:, length:]).astype(BF16)
+    packet_ref[:, :half] = (keys_turned[:, :half] - change[:, :half]).astype(BF16)
+    packet_ref[:, half:length] = (keys_turned[:, half:] - later[:, half + head_size :]).astype(BF16)
+    packet_ref[:, length:wide_size] = (identity - change[:, half:]).astype(BF16)
     copies[3].wait()
     ones_ref[:, head_size:] = jnp.ones((length, head_size), BF16)
     for part in range(length // head_size):
@@ -137,6 +139,25 @@
         ]
 
 
+def solve_rows(partial_ref, reflect_ref):
+    length, head_size = reflect_ref.shape
+    half = length // 2
+    second = halves(partial_ref[:, :half])
+    across = halves(partial_ref[:, half:length])
+    facing = partial_ref[:, length : 2 * length]
+    upper = partial_ref[:, 2 * length :]
+    reflect = reflect_ref[half:, :].astype(F32)
+    tall = jnp.concatenate([facing[:, :half], reflect, facing[:, half:]], axis=1)
+    lower = dot_halves(second, halves(tall))
+    bridge = dot_halves(second, across)
+    lower_left = lower[:, : half + head_size] - dot_halves(halves(bridge), halves(upper))
+    top = [upper[:, :half], jnp.zeros((half, half), F32), upper[:, half:]]
+    bottom = [lower_left[:, :half], lower[:, half + head_size :], lower_left[:, half:]]
+    return halves(
+        jnp.concatenate([jnp.concatenate(top, axis=1), jnp.concatenate(bottom, axis=1)], axis=0)
+    )
+
+
 def lane_pieces(scores, size):
     return [score[:, i : i + size] for score in scores for i in range(0, score.shape[1], size)]
 
@@ -156,15 +177,10 @@
     return rough * (2.0 - value * rough)
 
 
-def query_kernel(heads, longest, *refs):
-    docs_hbm, queries_ref, both_ref, ones_ref, solved_ref, gain_ref = refs[:6]
-    turned_ref, peak_ref, total_ref, weighted_ref, present_ref, docs_ref, docs_sem = refs[-7:]
-    if docs_hbm is not None:
-        docs_copy = pltpu.make_async_copy(docs_hbm, docs_ref, docs_sem)
-        docs_copy.start()
+def query_heads(heads, queries_ref, both_ref, ones_ref, solved, gain_ref, state_refs):
+    turned_ref, peak_ref, total_ref, weighted_ref = state_refs
     length = ones_ref.shape[0]
     head_size = ones_ref.shape[1] // 2
-    wide_size = length + head_size
     rate = math.log2(math.e) * head_size ** (-0.5)
     rows = lax.broadcasted_iota(jnp.int32, (length, length), 0)
     columns = lax.broadcasted_iota(jnp.int32, (length, length), 1)
@@ -172,14 +188,12 @@
     gain = jnp.where(visible, gain_ref[0:1, :], 0.0)
     hidden = jnp.where(visible, 0.0, -1e30)
     both = both_ref[...]
-    solved_high = solved_ref[:, :wide_size]
-    solved_low = solved_ref[:, wide_size:]
     values = ones_ref[...]
     for head in heads:
         span = slice(head * head_size, (head + 1) * head_size)
         queries = queries_ref[:, span]
         faced = dot(queries, both)
-        change = dot_halves(halves(faced[:, :length] * gain), (solved_high, solved_low))
+        change = dot_halves(halves(faced[:, :length] * gain), solved)
         scores = (faced[:, length:] - change[:, :length]) + hidden
         turned_ref[:, span] = (queries.astype(F32) - change[:, length:]).astype(BF16)
         peak = jnp.broadcast_to(jnp.max(scores, axis=1, keepdims=True), (length, head_size))
@@ -187,26 +201,44 @@
         peak_ref[:, span] = peak
         weighted_ref[:, span] = sums[:, :head_size]
         total_ref[:, span] = sums[:, head_size:]
-    if docs_hbm is not None:
-        docs_copy.wait()
-        block = lax.axis_index("outer") * lax.axis_size("inner") + lax.axis_index("inner")
-        own_doc = docs_ref[block]
-        present = jnp.int32(0)
-        for distance in range(1, longest):
-            source = block - distance
-            same = (source >= 0) & (docs_ref[jnp.maximum(source, 0)] == own_doc)
-            present = present + same.astype(jnp.int32)
-        present_ref[...] = jnp.full(present_ref.shape, present, jnp.int32)
-
-
-def other_queries(heads, longest, *refs):
-    for done_ref, state_ref in zip(refs[5:9], refs[9:13]):
+
+
+def first_queries(heads, longest, docs_hbm, *refs):
+    queries_ref, both_ref, ones_ref, partial_ref, reflect_ref, gain_ref = refs[:6]
+    state_refs = refs[6:10]
+    present_ref, solved_ref, docs_ref, docs_sem = refs[10:]
+    docs_copy = pltpu.make_async_copy(docs_hbm, docs_ref, docs_sem)
+    docs_copy.start()
+    solved = solve_rows(partial_ref, reflect_ref)
+    wide_size = solved[0].shape[1]
+    solved_ref[:, :wide_size] = solved[0]
+    solved_ref[:, wide_size:] = solved[1]
+    query_heads(heads, queries_ref, both_ref, ones_ref, solved, gain_ref, state_refs)
+    docs_copy.wait()
+    block = lax.axis_index("outer") * lax.axis_size("inner") + lax.axis_index("inner")
+    own_doc = docs_ref[block]
+    present = jnp.int32(0)
+    for distance in range(1, longest):
+        source = block - distance
+        same = (source >= 0) & (docs_ref[jnp.maximum(source, 0)] == own_doc)
+        present = present + same.astype(jnp.int32)
+    state = 2 * present + block % 2
+    present_ref[...] = jnp.full(present_ref.shape, state, jnp.int32)
+
+
+def other_queries(heads, *refs):
+    queries_ref, both_ref, ones_ref, solved_ref, gain_ref = refs[:5]
+    state_refs = refs[9:]
+    for done_ref, state_ref in zip(refs[5:9], state_refs):
         state_ref[:, : done_ref.shape[1]] = done_ref[...]
-    query_kernel(heads, longest, None, *refs, None, None, None)
-
-
-def is_odd():
-    return (lax.axis_index("inner") % 2) == 1
+    wide_size = solved_ref.shape[1] // 2
+    solved = (solved_ref[:, :wide_size], solved_ref[:, wide_size:])
+    query_heads(heads, queries_ref, both_ref, ones_ref, solved, gain_ref, state_refs)
+
+
+def present_and_odd(present_ref):
+    state = present_ref[0, 0]
+    return state // 2, state % 2 == 1
 
 
 def put_out(out_ref, out_hbm, out_sems, head, head_size):
@@ -264,25 +296,31 @@
     values_ref[slot, rows, head_size:] = jnp.ones((length, head_size), BF16)
 
 
-def nearest_kernel(head_count, present_ref, mixed_ref, *refs):
+def nearest(old_refs, new_refs, packet_ref, values_ref, out_refs):
+    packet = packet_ref[...]
+    length = values_ref.shape[1]
+    head_count = old_refs[0].shape[1] // packet.shape[0]
+    store_values(values_ref, 0, 0, packet, length)
+    attend(head_count, old_refs, new_refs, [packet[:, :length]], values_ref[0], out_refs)
+
+
+def nearest_kernel(head_count, present_ref, beside_ref, *refs):
     old_refs, new_refs = refs[:4], refs[4:7]
     out_hbm, out_ref, values_ref, out_sems = refs[7:]
     out_refs = (out_ref, out_hbm, out_sems)
-    length = out_ref.shape[0]
-    present = jnp.max(present_ref[...])
-    odd = is_odd()
-
-    def nearest(out):
-        packet = mixed_ref[...]
-        store_values(values_ref, 0, 0, packet, length)
-        attend(head_count, old_refs, new_refs, [packet[:, :length]], values_ref[0], out)
+    present, odd = present_and_odd(present_ref)
 
     @pl.when(present == 0)
     def _():
         finish(head_count, old_refs[2:], out_refs)
 
-    pl.when(odd & (present == 1))(lambda: nearest(out_refs))
-    pl.when(odd & (present > 1))(lambda: nearest(None))
+    @pl.when(odd & (present == 1))
+    def _():
+        nearest(old_refs, new_refs, beside_ref, values_ref, out_refs)
+
+    @pl.when(odd & (present > 1))
+    def _():
+        nearest(old_refs, new_refs, beside_ref, values_ref, None)
 
     @pl.when(jnp.logical_not(odd) & (present > 0))
     def _():
@@ -291,27 +329,23 @@
 
 
 def earlier_kernel(head_count, longest, present_ref, *refs):
-    packet_refs = refs[: longest - 1]
-    state_refs = refs[longest - 1 : longest + 3]
+    packet_refs = refs[:longest]
+    state_refs = refs[longest : longest + 4]
     out_hbm, out_ref, keys_ref, values_ref, out_sems = refs[-5:]
     out_refs = (out_ref, out_hbm, out_sems)
-    present = jnp.max(present_ref[...])
+    present, odd = present_and_odd(present_ref)
     length = out_ref.shape[0]
     head_size = out_ref.shape[1] // head_count
     wide_size = length + head_size
-    odd = is_odd()
     steps = longest // 2 - 1
-    apart_refs, swapped_refs, mixed_ref = (
-        packet_refs[:steps],
-        packet_refs[steps : 2 * steps],
-        packet_refs[2 * steps],
-    )
+    apart_refs, swapped_refs = packet_refs[:steps], packet_refs[steps : 2 * steps]
+    mixed_ref, beside_ref = packet_refs[2 * steps :]
     slots = values_ref.shape[0]
 
     def packet_of(distance, known_odd):
         if distance % 2 == 0:
             return apart_refs[distance // 2 - 1][...]
-        odd_ref = mixed_ref if distance == 1 else swapped_refs[(distance - 1) // 2 - 1]
+        odd_ref = beside_ref if distance == 1 else swapped_refs[(distance - 1) // 2 - 1]
         even_ref = mixed_ref if distance == longest - 1 else swapped_refs[(distance + 1) // 2 - 1]
         if known_odd is None:
             return jnp.where(odd, odd_ref[...], even_ref[...])
@@ -397,19 +431,19 @@
     params = pltpu.CompilerParams(vmem_limit_bytes=VMEM_LIMIT)
     shape = jax.ShapeDtypeStruct
     hbm = pl.BlockSpec(memory_space=pltpu.HBM)
-    packet, solved, gain, both, ones = pl.pallas_call(
+    packet, partial, gain, both, ones, reflect_rows = pl.pallas_call(
         key_kernel,
         out_shape=(
             shape((head_size, wide_size + length), BF16),
-            shape((length, 2 * wide_size), BF16),
+            shape((length // 2, 3 * length), F32),
             shape((8, length), F32),
             shape((head_size, 2 * length), BF16),
             shape((length, 2 * head_size), BF16),
+            shape((length, head_size), BF16),
         ),
         in_specs=[hbm] * 4,
-        out_specs=tuple(vmem(5)),
+        out_specs=tuple(vmem(6)),
         scratch_shapes=[
-            pltpu.VMEM((length, head_size), BF16),
             pltpu.VMEM((length, head_size), BF16),
             pltpu.VMEM((1, length), F32),
             pltpu.SemaphoreType.DMA((4,)),
@@ -423,7 +457,7 @@
     apart = [permuted(packet, lambda i, s=s: i + 2 * s) for s in range(1, longest // 2)]
     wide = shape(queries.shape, F32)
     state_shapes = (shape(queries.shape, BF16), wide, wide, wide)
-    first = max(1, head_count // 4)
+    first = 1
     first_shapes = [shape((length, first * head_size), part.dtype) for part in state_shapes]
 
     def query_cost(heads):
@@ -433,11 +467,15 @@
             transcendentals=heads * length * length,
         )
 
-    *state, present = pl.pallas_call(
-        functools.partial(query_kernel, range(first), longest),
-        out_shape=(*first_shapes, shape((8, 128), jnp.int32)),
-        in_specs=[hbm] + vmem(5),
-        out_specs=tuple(vmem(5)),
+    *state, present, solved = pl.pallas_call(
+        functools.partial(first_queries, range(first), longest),
+        out_shape=(
+            *first_shapes,
+            shape((8, 128), jnp.int32),
+            shape((length, 2 * wide_size), BF16),
+        ),
+        in_specs=[hbm] + vmem(6),
+        out_specs=tuple(vmem(6)),
         scratch_shapes=[
             pltpu.SMEM(doc_of_block.shape, jnp.int32),
             pltpu.SemaphoreType.DMA(()),
@@ -445,11 +483,14 @@
         compiler_params=params,
         cost_estimate=query_cost(first),
         name="first_queries",
-    )(in_hbm(doc_of_block), queries, both, ones, solved, gain)
+    )(in_hbm(doc_of_block), queries, both, ones, partial, reflect_rows, gain)
     mixed_packet, state[0] = lax.optimization_barrier((packet, state[0]))
+    beside = permuted(mixed_packet, lambda i: i ^ 1)
     mixed = permuted(mixed_packet, lambda i: i + longest - 1 if i % 2 else i + 1)
+    slots = (longest - 1 + GROUP - 1) // GROUP
+    one_values = pltpu.VMEM((1, length, 2 * head_size), BF16)
     state = pl.pallas_call(
-        functools.partial(other_queries, range(first, head_count), longest),
+        functools.partial(other_queries, range(first, head_count)),
         out_shape=state_shapes,
         in_specs=vmem(9),
         out_specs=tuple(vmem(4)),
@@ -461,7 +502,6 @@
     state = [turned, *state[1:]]
     swapped = [permuted(moved, lambda i: i ^ 1) for moved in apart]
     out_shape = shape(queries.shape, BF16)
-    slots = (longest - 1 + GROUP - 1) // GROUP
     out_scratch = [pltpu.VMEM(queries.shape, BF16), pltpu.SemaphoreType.DMA((head_count,))]
     sums, started = state[1:], []
     if slots == 1:
@@ -472,7 +512,7 @@
             out_specs=(*vmem(3), hbm),
             scratch_shapes=[
                 out_scratch[0],
-                pltpu.VMEM((1, length, 2 * head_size), BF16),
+                one_values,
                 out_scratch[1],
             ],
             compiler_params=params,
@@ -482,14 +522,14 @@
                 transcendentals=head_count * length * length,
             ),
             name="nearest_block",
-        )(present, mixed, *state)
+        )(present, beside, *state)
         started = [in_hbm(out)]
     return pl.pallas_call(
         functools.partial(earlier_kernel, head_count, longest),
         out_shape=out_shape,
-        in_specs=vmem(longest - 1 + 5) + [hbm] * len(started),
+        in_specs=vmem(longest + 5) + [hbm] * len(started),
         out_specs=hbm,
-        input_output_aliases={longest + 4: 0} if started else {},
+        input_output_aliases={longest + 5: 0} if started else {},
         scratch_shapes=[
             out_scratch[0],
             pltpu.VMEM((slots, head_size, GROUP * length), BF16),
@@ -503,7 +543,7 @@
             transcendentals=3 * head_count * length * length,
         ),
         name="earlier_blocks",
-    )(present, *apart, *swapped, mixed, turned, *sums, *started)
+    )(present, *apart, *swapped, mixed, beside, turned, *sums, *started)
 
 
 def solution(mesh):

time: 17.6 us -> 17.1 us (0.972); the launches traced: 17.9 us -> 17 us
  waiting for transfers between devices: 1.89 us -> 0.91 us
  Pallas kernels: 9.95 us -> 10.3 us
  starting transfers between devices: 5.83 us -> 5.53 us
    ppermute x3 -> x4, waiting for transfers between devices: 1.89 us -> 0.91 us  [permuted(): lax.ppermute(value, AXES, [(i, target(i) % count) for i in range(count)])]
    pallas_call x2, Pallas kernels: 3.89 us -> 4.8 us  [the longest x1 3.18 us: local(): pl.pallas_call(functools.partial(other_queries, range(first, head_count))...]
    ppermute x3 -> x4, starting transfers between devices: 5.83 us -> 5.53 us  [permuted(): lax.ppermute(value, AXES, [(i, target(i) % count) for i in range(count)])]
    pallas_call x1, Pallas kernels: 3.46 us -> 3.23 us  [local(): pl.pallas_call(key_kernel, out_shape=(shape((head_size, wide_size + lengt...]
  transfers between devices with their start and end apart: 3 -> 4, of which waited for: 1 -> 1; matrix products, arithmetic and copies ran while one was open for 0% -> 0% of each run, Pallas kernels for 34% -> 40%
where the time goes in v4:
time: 17.1 us; the launch traced here: 17 us
  Pallas kernels  10.3 us (60%)
  starting transfers between devices  5.53 us (32%)
  waiting for transfers between devices  0.91 us (5%)
  between operations  0.21 us (1%)
    ppermute x4, starting transfers between devices, permuted(): lax.ppermute(value, AXES, [(i, target(i) % count) for i in range(count)])  5.53 us
    pallas_call x1, Pallas kernels, local(): pl.pallas_call(key_kernel, out_shape=(shape((head_size, wide_size + lengt...  3.23 us
    pallas_call x1, Pallas kernels, local(): pl.pallas_call(functools.partial(other_queries, range(first, head_count))...  3.18 us
    pallas_call x1, Pallas kernels, local(): pl.pallas_call(functools.partial(nearest_kernel, head_count), out_shape=(...  1.97 us
    pallas_call x1, Pallas kernels, local(): pl.pallas_call(functools.partial(first_queries, range(first), longest), o...  1.62 us
    ppermute x4, waiting for transfers between devices, permuted(): lax.ppermute(value, AXES, [(i, target(i) % count) for i in range(count)])  0.91 us
  transfers between devices with their start and end apart: 4, of which 1 were waited for; matrix products, arithmetic and copies ran while one was open for 0% of the time, Pallas kernels for 40%

profile of v4, /device:TPU:1, one launch (start us, length us, event | category | flops | bytes accessed | tf_op | source)
XLA Modules:
  0.0 17.0 jit_solution(6227873095826270110)
XLA Ops:
  0.0 0.0 copy-start
  0.0 3.2 %key_side.1 = (bf16[128,640]{1,0:T(8,128)(2,1)S(1)}, f32[128,768]{1,0:T(8,128)S(1)}, f32[8,256]{1,0:T(8,128)S(1)}, bf16[128,512]{1,0:T(8,128)(2,1)S(1)}, bf16[25...) custom-call(bf16[256,128]{1,0:T(8,128)(2,1)} %reflect_hbm.1, bf16[256,128]{1,0:T(8,128)(2,1)} %keys_hbm.1, ...), custom_call_target="tpu_custom_call" | custom-call | flops 671088640 | bytes 524288 | tf_op jit(solution)/shard_map/key_side/pallas_call | solution.py:434
  3.2 2.1 %collective-permute-start = (bf16[128,640]{1,0:T(8,128)(2,1)S(1)}, bf16[128,640]{1,0:T(8,128)(2,1)S(1)}, u32[]{:S(2)}, u32[]{:S(2)}) collective-permute-start(bf16[128,640]{1,0:T(8,128)(2,1)S(1)} %get-tuple-element.44), channel_id=1, source_target_pairs={{0,2},{1,3},{2,4},{3,5},{4,6},{5,7},{6,8},{7,9},{8,10},{9,11},{10,... | collective-permute-start | bytes 491528 | tf_op jit(solution)/shard_map/ppermute | solution.py:423
  5.4 0.0 copy-done
  5.4 1.6 %first_queries.1 = (bf16[256,128]{1,0:T(8,128)(2,1)S(1)}, f32[256,128]{1,0:T(8,128)S(1)}, f32[256,128]{1,0:T(8,128)S(1)}, f32[256,128]{1,0:T(8,128)S(1)}, s32[8,...) custom-call(s32[32]{0:T(128)} %docs_hbm.1, bf16[256,1024]{1,0:T(8,128)(2,1)S(1)} %copy-done, ...), custom_call_target="tpu_custom_call" | custom-call | flops 167772160 | bytes 1048576 | tf_op jit(solution)/shard_map/first_queries/pallas_call | solution.py:470
  7.0 1.0 %collective-permute-start.3 = (bf16[128,640]{1,0:T(8,128)(2,1)S(1)}, bf16[128,640]{1,0:T(8,128)(2,1)S(1)}, u32[]{:S(2)}, u32[]{:S(2)}) collective-permute-start(bf16[128,640]{1,0:T(8,128)(2,1)S(1)} %get-tuple-element.44), channel_id=1, source_target_pairs={{0,1},{1,0},{2,3},{3,2},{4,5},{5,4},{6,7},{7,6},{8,9},{9,8},{10,11... | collective-permute-start | bytes 491528 | tf_op jit(solution)/shard_map/ppermute | solution.py:423
  8.0 1.2 %collective-permute-start.2 = (bf16[128,640]{1,0:T(8,128)(2,1)S(1)}, bf16[128,640]{1,0:T(8,128)(2,1)S(1)}, u32[]{:S(2)}, u32[]{:S(2)}) collective-permute-start(bf16[128,640]{1,0:T(8,128)(2,1)S(1)} %get-tuple-element.44), channel_id=1, source_target_pairs={{0,1},{1,4},{2,3},{3,6},{4,5},{5,8},{6,7},{7,10},{8,9},{9,12},{10,... | collective-permute-start | bytes 491528 | tf_op jit(solution)/shard_map/ppermute | solution.py:423
  9.2 3.2 %other_queries.1 = (bf16[256,1024]{1,0:T(8,128)(2,1)S(1)}, f32[256,1024]{1,0:T(8,128)S(1)}, f32[256,1024]{1,0:T(8,128)S(1)}, f32[256,1024]{1,0:T(8,128)S(1)}) custom-call(bf16[256,1024]{1,0:T(8,128)(2,1)S(1)} %copy-done, bf16[128,512]{1,0:T(8,128)(2,1)S(1)} %get-tuple-element.29.refs_1_, bf16[256,256]{1,0:T(8,128)(2,1)S(1)} %get-tuple-element.30.refs_2_, ...), custom_call_target="tpu_custom_call" | custom-call | flops 1174405120 | bytes 7340032 | tf_op jit(solution)/shard_map/other_queries/pallas_call | solution.py:492
  12.4 0.9 %collective-permute-done.refs_0_ = bf16[128,640]{1,0:T(8,128)(2,1)S(1)} collective-permute-done((bf16[128,640]{1,0:T(8,128)(2,1)S(1)}, bf16[128,640]{1,0:T(8,128)(2,1)S(1)}, u32[]{:S(2)}, u32[]{:S(2)}) %collective-permute-start) | collective-permute-done | bytes 163872 | tf_op jit(solution)/shard_map/ppermute | solution.py:423
  13.3 1.2 %collective-permute-start.1 = (bf16[128,640]{1,0:T(8,128)(2,1)S(1)}, bf16[128,640]{1,0:T(8,128)(2,1)S(1)}, u32[]{:S(2)}, u32[]{:S(2)}) collective-permute-start(bf16[128,640]{1,0:T(8,128)(2,1)S(1)} %collective-permute-done.refs_0_), channel_id=1, source_target_pairs={{0,1},{1,0},{2,3},{3,2},{4,5},{5,4},{6,7},{7,6},{8,9},{9,8},{10,11... | collective-permute-start | bytes 491528 | tf_op jit(solution)/shard_map/ppermute | solution.py:423
  14.5 0.0 collective-permute-done.3.beside_ref.refs_3_
  14.5 2.0 %nearest_block.1 = (f32[256,1024]{1,0:T(8,128)S(1)}, f32[256,1024]{1,0:T(8,128)S(1)}, f32[256,1024]{1,0:T(8,128)S(1)}, bf16[256,1024]{1,0:T(8,128)(2,1)}) custom-call(s32[8,128]{1,0:T(8,128)S(1)} %get-tuple-element.34.present_ref, bf16[128,640]{1,0:T(8,128)(2,1)S(1)} %collective-permute-done.3.beside_ref.refs_3_, ...), custom_call_target="tpu_custom_call" | custom-call | flops 268435456 | bytes 2097152 | tf_op jit(solution)/shard_map/nearest_block/pallas_call | solution.py:508
  16.5 0.0 collective-permute-done.2.refs_2_
  16.5 0.0 collective-permute-done.1.refs_1_
  16.5 0.3 %earlier_blocks.1 = bf16[256,1024]{1,0:T(8,128)(2,1)} custom-call(s32[8,128]{1,0:T(8,128)S(1)} %get-tuple-element.34.present_ref, bf16[128,640]{1,0:T(8,128)(2,1)S(1)} %collective-permute-done.refs_0_, bf16[128,640]{1,0:T(8,128)(2,1)S(1)} %collective-permute-done.1.refs_1_, ...), custom_call_target="tpu_custom_call", output_to_operand_aliasing={{}: (9, {})} | custom-call | flops 805306368 | bytes 8388608 | tf_op jit(solution)/shard_map/earlier_blocks/pallas_call | solution.py:527
Async XLA Ops:
  0.0 5.4 %copy-start = (bf16[256,1024]{1,0:T(8,128)(2,1)S(1)}, bf16[256,1024]{1,0:T(8,128)(2,1)}, u32[]{:S(2)}) copy-start(bf16[256,1024]{1,0:T(8,128)(2,1)} %refs_0_.3) | copy-start | bytes 1572868
  3.2 10.0 %collective-permute-start = (bf16[128,640]{1,0:T(8,128)(2,1)S(1)}, bf16[128,640]{1,0:T(8,128)(2,1)S(1)}, u32[]{:S(2)}, u32[]{:S(2)}) collective-permute-start(bf16[128,640]{1,0:T(8,128)(2,1)S(1)} %get-tuple-element.44), channel_id=1, source_target_pairs={{0,2},{1,3},{2,4},{3,5},{4,6},{5,7},{6,8},{7,9},{8,10},{9,11},{10,... | collective-permute-start | bytes 491528 | tf_op jit(solution)/shard_map/ppermute | solution.py:423
  7.0 7.5 %collective-permute-start.3 = (bf16[128,640]{1,0:T(8,128)(2,1)S(1)}, bf16[128,640]{1,0:T(8,128)(2,1)S(1)}, u32[]{:S(2)}, u32[]{:S(2)}) collective-permute-start(bf16[128,640]{1,0:T(8,128)(2,1)S(1)} %get-tuple-element.44), channel_id=1, source_target_pairs={{0,1},{1,0},{2,3},{3,2},{4,5},{5,4},{6,7},{7,6},{8,9},{9,8},{10,11... | collective-permute-start | bytes 491528 | tf_op jit(solution)/shard_map/ppermute | solution.py:423
  8.0 8.5 %collective-permute-start.2 = (bf16[128,640]{1,0:T(8,128)(2,1)S(1)}, bf16[128,640]{1,0:T(8,128)(2,1)S(1)}, u32[]{:S(2)}, u32[]{:S(2)}) collective-permute-start(bf16[128,640]{1,0:T(8,128)(2,1)S(1)} %get-tuple-element.44), channel_id=1, source_target_pairs={{0,1},{1,4},{2,3},{3,6},{4,5},{5,8},{6,7},{7,10},{8,9},{9,12},{10,... | collective-permute-start | bytes 491528 | tf_op jit(solution)/shard_map/ppermute | solution.py:423
  13.3 3.2 %collective-permute-start.1 = (bf16[128,640]{1,0:T(8,128)(2,1)S(1)}, bf16[128,640]{1,0:T(8,128)(2,1)S(1)}, u32[]{:S(2)}, u32[]{:S(2)}) collective-permute-start(bf16[128,640]{1,0:T(8,128)(2,1)S(1)} %collective-permute-done.refs_0_), channel_id=1, source_target_pairs={{0,1},{1,0},{2,3},{3,2},{4,5},{5,4},{6,7},{7,6},{8,9},{9,8},{10,11... | collective-permute-start | bytes 491528 | tf_op jit(solution)/shard_map/ppermute | solution.py:423

commit v5 on v4

--- a/solution.py
+++ b/solution.py
@@ -203,16 +203,25 @@
         total_ref[:, span] = sums[:, head_size:]
 
 
-def first_queries(heads, longest, docs_hbm, *refs):
+def first_queries(heads, *refs):
     queries_ref, both_ref, ones_ref, partial_ref, reflect_ref, gain_ref = refs[:6]
-    state_refs = refs[6:10]
-    present_ref, solved_ref, docs_ref, docs_sem = refs[10:]
-    docs_copy = pltpu.make_async_copy(docs_hbm, docs_ref, docs_sem)
-    docs_copy.start()
+    *state_refs, solved_ref = refs[6:]
     solved = solve_rows(partial_ref, reflect_ref)
     wide_size = solved[0].shape[1]
     solved_ref[:, :wide_size] = solved[0]
     solved_ref[:, wide_size:] = solved[1]
+    query_heads(heads, queries_ref, both_ref, ones_ref, solved, gain_ref, state_refs)
+
+
+def other_queries(heads, longest, docs_hbm, *refs):
+    queries_ref, both_ref, ones_ref, solved_ref, gain_ref = refs[:5]
+    *state_refs, present_ref, docs_ref, docs_sem = refs[9:]
+    docs_copy = pltpu.make_async_copy(docs_hbm, docs_ref, docs_sem)
+    docs_copy.start()
+    for done_ref, state_ref in zip(refs[5:9], state_refs):
+        state_ref[:, : done_ref.shape[1]] = done_ref[...]
+    wide_size = solved_ref.shape[1] // 2
+    solved = (solved_ref[:, :wide_size], solved_ref[:, wide_size:])
     query_heads(heads, queries_ref, both_ref, ones_ref, solved, gain_ref, state_refs)
     docs_copy.wait()
     block = lax.axis_index("outer") * lax.axis_size("inner") + lax.axis_index("inner")
@@ -226,16 +235,6 @@
     present_ref[...] = jnp.full(present_ref.shape, state, jnp.int32)
 
 
-def other_queries(heads, *refs):
-    queries_ref, both_ref, ones_ref, solved_ref, gain_ref = refs[:5]
-    state_refs = refs[9:]
-    for done_ref, state_ref in zip(refs[5:9], state_refs):
-        state_ref[:, : done_ref.shape[1]] = done_ref[...]
-    wide_size = solved_ref.shape[1] // 2
-    solved = (solved_ref[:, :wide_size], solved_ref[:, wide_size:])
-    query_heads(heads, queries_ref, both_ref, ones_ref, solved, gain_ref, state_refs)
-
-
 def present_and_odd(present_ref):
     state = present_ref[0, 0]
     return state // 2, state % 2 == 1
@@ -246,11 +245,11 @@
     return pltpu.make_async_copy(out_ref.at[:, span], out_hbm.at[:, span], out_sems.at[head])
 
 
-def attend(head_count, state_refs, new_refs, all_keys, values, out_refs):
+def attend(heads, state_refs, new_refs, all_keys, values, out_refs):
     turned_ref, peak_ref, total_ref, weighted_ref = state_refs
-    head_size = turned_ref.shape[1] // head_count
+    head_size = values.shape[1] // 2
     rate = math.log2(math.e) * head_size ** (-0.5)
-    for head in range(head_count):
+    for head in heads:
         span = slice(head * head_size, (head + 1) * head_size)
         old_peak = peak_ref[:, span]
         scores = [dot(turned_ref[:, span], keys) for keys in all_keys]
@@ -261,12 +260,13 @@
         weighted = weighted_ref[:, span] * factor + sums[:, :head_size]
         if out_refs is not None:
             out_refs[0][:, span] = (weighted * reciprocal(total)).astype(BF16)
-            put_out(*out_refs, head, head_size).start()
+            if len(out_refs) > 1:
+                put_out(*out_refs, head, head_size).start()
         else:
             for new_ref, new in zip(new_refs, (peak, total, weighted)):
                 new_ref[:, span] = new
-    if out_refs is not None:
-        wait_out(head_count, out_refs)
+    if out_refs is not None and len(out_refs) > 1:
+        wait_out(heads, out_refs, head_size)
 
 
 def finish(head_count, sum_refs, out_refs):
@@ -276,12 +276,11 @@
         span = slice(head * head_size, (head + 1) * head_size)
         out_refs[0][:, span] = (weighted_ref[:, span] * reciprocal(total_ref[:, span])).astype(BF16)
         put_out(*out_refs, head, head_size).start()
-    wait_out(head_count, out_refs)
-
-
-def wait_out(head_count, out_refs):
-    head_size = out_refs[0].shape[1] // head_count
-    for head in range(head_count):
+    wait_out(range(head_count), out_refs, head_size)
+
+
+def wait_out(heads, out_refs, head_size):
+    for head in heads:
         put_out(*out_refs, head, head_size).wait()
 
 
@@ -296,31 +295,55 @@
     values_ref[slot, rows, head_size:] = jnp.ones((length, head_size), BF16)
 
 
-def nearest(old_refs, new_refs, packet_ref, values_ref, out_refs):
+def nearest(heads, old_refs, new_refs, packet_ref, values_ref, out_refs):
     packet = packet_ref[...]
     length = values_ref.shape[1]
-    head_count = old_refs[0].shape[1] // packet.shape[0]
     store_values(values_ref, 0, 0, packet, length)
-    attend(head_count, old_refs, new_refs, [packet[:, :length]], values_ref[0], out_refs)
-
-
-def nearest_kernel(head_count, present_ref, beside_ref, *refs):
+    attend(heads, old_refs, new_refs, [packet[:, :length]], values_ref[0], out_refs)
+
+
+def is_first_odd():
+    return (lax.axis_index("outer") == 0) & (lax.axis_index("inner") == 1)
+
+
+def early_kernel(heads, present_ref, beside_ref, *refs):
+    *state_refs, done_ref, values_ref = refs
+    present, _ = present_and_odd(present_ref)
+
+    @pl.when(is_first_odd() & (present == 1))
+    def _():
+        nearest(heads, state_refs, None, beside_ref, values_ref, (done_ref,))
+
+
+def nearest_kernel(head_count, early_heads, present_ref, beside_ref, done_ref, *refs):
     old_refs, new_refs = refs[:4], refs[4:7]
     out_hbm, out_ref, values_ref, out_sems = refs[7:]
     out_refs = (out_ref, out_hbm, out_sems)
     present, odd = present_and_odd(present_ref)
+    first_odd = is_first_odd()
+    heads = range(head_count)
 
     @pl.when(present == 0)
     def _():
         finish(head_count, old_refs[2:], out_refs)
 
-    @pl.when(odd & (present == 1))
+    @pl.when(first_odd & (present == 1))
     def _():
-        nearest(old_refs, new_refs, beside_ref, values_ref, out_refs)
+        head_size = beside_ref.shape[0]
+        done_refs = (done_ref, out_hbm, out_sems)
+        for head in heads[:early_heads]:
+            put_out(*done_refs, head, head_size).start()
+        if early_heads < head_count:
+            nearest(heads[early_heads:], old_refs, new_refs, beside_ref, values_ref, out_refs)
+        wait_out(heads[:early_heads], done_refs, head_size)
+
+    @pl.when(odd & (present == 1) & jnp.logical_not(first_odd))
+    def _():
+        nearest(heads, old_refs, new_refs, beside_ref, values_ref, out_refs)
 
     @pl.when(odd & (present > 1))
     def _():
-        nearest(old_refs, new_refs, beside_ref, values_ref, None)
+        nearest(heads, old_refs, new_refs, beside_ref, values_ref, None)
 
     @pl.when(jnp.logical_not(odd) & (present > 0))
     def _():
@@ -375,16 +398,31 @@
                 store_values(values_ref, index // GROUP, index % GROUP, packet, length)
         return all_keys
 
+    def take(first, last, known_odd):
+        keys = collect(first, last, known_odd)
+        values = values_ref[0, : len(keys) * length, :]
+        attend(range(head_count), state_refs, None, keys, values, out_refs)
+
+    def choose(first, last, known_odd):
+        if first == last:
+            take(2 if known_odd else 1, last, known_odd)
+        else:
+            middle = (first + last + 1) // 2
+            lax.cond(
+                present >= middle,
+                lambda: choose(middle, last, known_odd),
+                lambda: choose(first, middle - 1, known_odd),
+            )
+
     if slots == 1:
-        for known_odd in (False, True):
-            first = 2 if known_odd else 1
-            for last in range(first, longest):
-
-                @pl.when((odd == known_odd) & (present == last))
-                def _(known_odd=known_odd, first=first, last=last):
-                    keys = collect(first, last, known_odd)
-                    values = values_ref[0, : len(keys) * length, :]
-                    attend(head_count, state_refs, None, keys, values, out_refs)
+
+        @pl.when(present > odd.astype(jnp.int32))
+        def _():
+            lax.cond(
+                odd,
+                lambda: choose(2, longest - 1, True),
+                lambda: choose(1, longest - 1, False),
+            )
 
     else:
 
@@ -397,7 +435,7 @@
         def visit(slot, blocks):
             keys = [keys_ref[slot, :, i * length : (i + 1) * length] for i in range(blocks)]
             values = values_ref[slot, : blocks * length, :]
-            attend(head_count, state_refs, state_refs[1:], keys, values, None)
+            attend(range(head_count), state_refs, state_refs[1:], keys, values, None)
 
         full = present // GROUP
 
@@ -457,7 +495,7 @@
     apart = [permuted(packet, lambda i, s=s: i + 2 * s) for s in range(1, longest // 2)]
     wide = shape(queries.shape, F32)
     state_shapes = (shape(queries.shape, BF16), wide, wide, wide)
-    first = 1
+    first = max(1, head_count // 4)
     first_shapes = [shape((length, first * head_size), part.dtype) for part in state_shapes]
 
     def query_cost(heads):
@@ -467,62 +505,70 @@
             transcendentals=heads * length * length,
         )
 
-    *state, present, solved = pl.pallas_call(
-        functools.partial(first_queries, range(first), longest),
-        out_shape=(
-            *first_shapes,
-            shape((8, 128), jnp.int32),
-            shape((length, 2 * wide_size), BF16),
-        ),
-        in_specs=[hbm] + vmem(6),
-        out_specs=tuple(vmem(6)),
+    *state, solved = pl.pallas_call(
+        functools.partial(first_queries, range(first)),
+        out_shape=(*first_shapes, shape((length, 2 * wide_size), BF16)),
+        in_specs=vmem(6),
+        out_specs=tuple(vmem(5)),
+        compiler_params=params,
+        cost_estimate=query_cost(first),
+        name="first_queries",
+    )(queries, both, ones, partial, reflect_rows, gain)
+    mixed_packet, state[0] = lax.optimization_barrier((packet, state[0]))
+    beside = permuted(mixed_packet, lambda i: i ^ 1)
+    mixed = permuted(mixed_packet, lambda i: i + longest - 1 if i % 2 else i + 1)
+    slots = (longest - 1 + GROUP - 1) // GROUP
+    one_values = pltpu.VMEM((1, length, 2 * head_size), BF16)
+    *state, present = pl.pallas_call(
+        functools.partial(other_queries, range(first, head_count), longest),
+        out_shape=(*state_shapes, shape((8, 128), jnp.int32)),
+        in_specs=[hbm] + vmem(9),
+        out_specs=tuple(vmem(5)),
         scratch_shapes=[
             pltpu.SMEM(doc_of_block.shape, jnp.int32),
             pltpu.SemaphoreType.DMA(()),
         ],
         compiler_params=params,
-        cost_estimate=query_cost(first),
-        name="first_queries",
-    )(in_hbm(doc_of_block), queries, both, ones, partial, reflect_rows, gain)
-    mixed_packet, state[0] = lax.optimization_barrier((packet, state[0]))
-    beside = permuted(mixed_packet, lambda i: i ^ 1)
-    mixed = permuted(mixed_packet, lambda i: i + longest - 1 if i % 2 else i + 1)
+        cost_estimate=query_cost(head_count - first),
+        name="other_queries",
+    )(in_hbm(doc_of_block), queries, both, ones, solved, gain, *state)
+    out_shape = shape(queries.shape, BF16)
     slots = (longest - 1 + GROUP - 1) // GROUP
     one_values = pltpu.VMEM((1, length, 2 * head_size), BF16)
-    state = pl.pallas_call(
-        functools.partial(other_queries, range(first, head_count)),
-        out_shape=state_shapes,
-        in_specs=vmem(9),
-        out_specs=tuple(vmem(4)),
-        compiler_params=params,
-        cost_estimate=query_cost(head_count - first),
-        name="other_queries",
-    )(queries, both, ones, solved, gain, *state)
-    *apart, turned = lax.optimization_barrier((*apart, state[0]))
-    state = [turned, *state[1:]]
+    out_scratch = [pltpu.VMEM(queries.shape, BF16), pltpu.SemaphoreType.DMA((head_count,))]
+    nearest_cost = pl.CostEstimate(
+        flops=head_count * 2 * length**3,
+        bytes_accessed=4 * length * length * head_count,
+        transcendentals=head_count * length * length,
+    )
+    turned = state[0]
+    *apart, present = lax.optimization_barrier((*apart, present))
+    early_heads = head_count
+    if slots == 1:
+        done = pl.pallas_call(
+            functools.partial(early_kernel, range(early_heads)),
+            out_shape=shape((length, early_heads * head_size), BF16),
+            in_specs=vmem(6),
+            out_specs=vmem(1)[0],
+            scratch_shapes=[one_values],
+            compiler_params=params,
+            cost_estimate=pl.CostEstimate(flops=0, bytes_accessed=0, transcendentals=0),
+            name="early_heads",
+        )(present, beside, *state)
+        *apart, done = lax.optimization_barrier((*apart, done))
     swapped = [permuted(moved, lambda i: i ^ 1) for moved in apart]
-    out_shape = shape(queries.shape, BF16)
-    out_scratch = [pltpu.VMEM(queries.shape, BF16), pltpu.SemaphoreType.DMA((head_count,))]
     sums, started = state[1:], []
     if slots == 1:
         *sums, out = pl.pallas_call(
-            functools.partial(nearest_kernel, head_count),
+            functools.partial(nearest_kernel, head_count, early_heads),
             out_shape=(*state_shapes[1:], out_shape),
-            in_specs=vmem(6),
+            in_specs=vmem(7),
             out_specs=(*vmem(3), hbm),
-            scratch_shapes=[
-                out_scratch[0],
-                one_values,
-                out_scratch[1],
-            ],
+            scratch_shapes=[out_scratch[0], one_values, out_scratch[1]],
             compiler_params=params,
-            cost_estimate=pl.CostEstimate(
-                flops=head_count * 2 * length**3,
-                bytes_accessed=4 * length * length * head_count,
-                transcendentals=head_count * length * length,
-            ),
+            cost_estimate=nearest_cost,
             name="nearest_block",
-        )(present, beside, *state)
+        )(present, beside, done, *state)
         started = [in_hbm(out)]
     return pl.pallas_call(
         functools.partial(earlier_kernel, head_count, longest),

time: 17.1 us -> 16.9 us (0.988)
  the two profiles are of different devices: /device:TPU:1 before, /device:TPU:0 now
where the time goes in v5:
time: 16.9 us; the launch traced here: 16.6 us
  Pallas kernels  8.77 us (52%)
  starting transfers between devices  4.09 us (24%)
  waiting for transfers between devices  3.5 us (21%)
  between operations  0.24 us (1%)
    ppermute x4, starting transfers between devices, permuted(): lax.ppermute(value, AXES, [(i, target(i) % count) for i in range(count)])  4.09 us
    ppermute x4, waiting for transfers between devices, permuted(): lax.ppermute(value, AXES, [(i, target(i) % count) for i in range(count)])  3.5 us
    pallas_call x1, Pallas kernels, local(): pl.pallas_call(key_kernel, out_shape=(shape((head_size, wide_size + lengt...  3.24 us
    pallas_call x1, Pallas kernels, local(): pl.pallas_call(functools.partial(other_queries, range(first, head_count),...  2.77 us
    pallas_call x1, Pallas kernels, local(): pl.pallas_call(functools.partial(first_queries, range(first)), out_shape=...  1.36 us
    pallas_call x1, Pallas kernels, local(): pl.pallas_call(functools.partial(nearest_kernel, head_count, early_heads)...  1.02 us
    pallas_call x1, Pallas kernels, local(): pl.pallas_call(functools.partial(earlier_kernel, head_count, longest), ou...  0.34 us
  transfers between devices with their start and end apart: 4, of which 1 were waited for; matrix products, arithmetic and copies ran while one was open for 0% of the time, Pallas kernels for 31%

profile of v5, /device:TPU:0, one launch (start us, length us, event | category | flops | bytes accessed | tf_op | source)
XLA Modules:
  0.0 16.6 jit_solution(10082656001348434445)
XLA Ops:
  0.0 0.0 copy-start
  0.0 3.2 %key_side.1 = (bf16[128,640]{1,0:T(8,128)(2,1)S(1)}, f32[128,768]{1,0:T(8,128)S(1)}, f32[8,256]{1,0:T(8,128)S(1)}, bf16[128,512]{1,0:T(8,128)(2,1)S(1)}, bf16[25...) custom-call(bf16[256,128]{1,0:T(8,128)(2,1)} %reflect_hbm.1, bf16[256,128]{1,0:T(8,128)(2,1)} %keys_hbm.1, ...), custom_call_target="tpu_custom_call" | custom-call | flops 671088640 | bytes 524288 | tf_op jit(solution)/shard_map/key_side/pallas_call | solution.py:472
  3.2 3.0 %collective-permute-start = (bf16[128,640]{1,0:T(8,128)(2,1)S(1)}, bf16[128,640]{1,0:T(8,128)(2,1)S(1)}, u32[]{:S(2)}, u32[]{:S(2)}) collective-permute-start(bf16[128,640]{1,0:T(8,128)(2,1)S(1)} %get-tuple-element.46), channel_id=1, source_target_pairs={{0,2},{1,3},{2,4},{3,5},{4,6},{5,7},{6,8},{7,9},{8,10},{9,11},{10,... | collective-permute-start | bytes 491528 | tf_op jit(solution)/shard_map/ppermute | solution.py:461
  6.3 0.0 copy-done
  6.3 1.4 %first_queries.1 = (bf16[256,256]{1,0:T(8,128)(2,1)S(1)}, f32[256,256]{1,0:T(8,128)S(1)}, f32[256,256]{1,0:T(8,128)S(1)}, f32[256,256]{1,0:T(8,128)S(1)}, bf16[256,768]{1,0:T(8,128)(2,1)S(1)}) custom-call(bf16[256,1024]{1,0:T(8,128)(2,1)S(1)} %copy-done, bf16[128,512]{1,0:T(8,128)(2,1)S(1)} %get-tuple-element.32.refs_1_, ...), custom_call_target="tpu_custom_call" | custom-call | flops 335544320 | bytes 2097152 | tf_op jit(solution)/shard_map/first_queries/pallas_call | solution.py:508
  7.6 0.1 collective-permute-start.1
  7.7 0.5 %collective-permute-start.3 = (bf16[128,640]{1,0:T(8,128)(2,1)S(1)}, bf16[128,640]{1,0:T(8,128)(2,1)S(1)}, u32[]{:S(2)}, u32[]{:S(2)}) collective-permute-start(bf16[128,640]{1,0:T(8,128)(2,1)S(1)} %get-tuple-element.46), channel_id=1, source_target_pairs={{0,1},{1,4},{2,3},{3,6},{4,5},{5,8},{6,7},{7,10},{8,9},{9,12},{10,... | collective-permute-start | bytes 491528 | tf_op jit(solution)/shard_map/ppermute | solution.py:461
  8.2 2.8 %other_queries.1 = (bf16[256,1024]{1,0:T(8,128)(2,1)S(1)}, f32[256,1024]{1,0:T(8,128)S(1)}, f32[256,1024]{1,0:T(8,128)S(1)}, f32[256,1024]{1,0:T(8,128)S(1)}, s32[8,128]{1,0:T(8,128)S(1)}) custom-call(s32[32]{0:T(128)} %docs_hbm.1, bf16[256,1024]{1,0:T(8,128)(2,1)S(1)} %copy-done, bf16[128,512]{1,0:T(8,128)(2,1)S(1)} %get-tuple-element.32.refs_1_, ...), custom_call_target="tpu_custom_call" | custom-call | flops 1006632960 | bytes 6291456 | tf_op jit(solution)/shard_map/other_queries/pallas_call | solution.py:522
  11.0 3.5 %collective-permute-done.refs_0_ = bf16[128,640]{1,0:T(8,128)(2,1)S(1)} collective-permute-done((bf16[128,640]{1,0:T(8,128)(2,1)S(1)}, bf16[128,640]{1,0:T(8,128)(2,1)S(1)}, u32[]{:S(2)}, u32[]{:S(2)}) %collective-permute-start) | collective-permute-done | bytes 163872 | tf_op jit(solution)/shard_map/ppermute | solution.py:461
  14.5 0.0 collective-permute-done.1.beside_ref.refs_3_
  14.5 0.5 %collective-permute-start.2 = (bf16[128,640]{1,0:T(8,128)(2,1)S(1)}, bf16[128,640]{1,0:T(8,128)(2,1)S(1)}, u32[]{:S(2)}, u32[]{:S(2)}) collective-permute-start(bf16[128,640]{1,0:T(8,128)(2,1)S(1)} %collective-permute-done.refs_0_), channel_id=1, source_target_pairs={{0,1},{1,0},{2,3},{3,2},{4,5},{5,4},{6,7},{7,6},{8,9},{9,8},{10,11... | collective-permute-start | bytes 491528 | tf_op jit(solution)/shard_map/ppermute | solution.py:461
  15.0 1.0 %nearest_block.1 = (f32[256,1024]{1,0:T(8,128)S(1)}, f32[256,1024]{1,0:T(8,128)S(1)}, f32[256,1024]{1,0:T(8,128)S(1)}, bf16[256,1024]{1,0:T(8,128)(2,1)}) custom-call(s32[8,128]{1,0:T(8,128)S(1)} %get-tuple-element.44.present_ref, bf16[128,640]{1,0:T(8,128)(2,1)S(1)} %collective-permute-done.1.beside_ref.refs_3_, bf16[256,1024]{1,0:T(8,128)(2,1)S(1)} %early_heads.1.done_ref, ...), custom_call_target="tpu_custom_call" | custom-call | flops 268435456 | bytes 2097152 | tf_op jit(solution)/shard_map/nearest_block/pallas_call | solution.py:562
  16.1 0.0 collective-permute-done.3.refs_2_
  16.1 0.0 collective-permute-done.2.refs_1_
  16.1 0.3 %earlier_blocks.1 = bf16[256,1024]{1,0:T(8,128)(2,1)} custom-call(s32[8,128]{1,0:T(8,128)S(1)} %get-tuple-element.44.present_ref, bf16[128,640]{1,0:T(8,128)(2,1)S(1)} %collective-permute-done.refs_0_, bf16[128,640]{1,0:T(8,128)(2,1)S(1)} %collective-permute-done.2.refs_1_, ...), custom_call_target="tpu_custom_call", output_to_operand_aliasing={{}: (9, {})} | custom-call | flops 805306368 | bytes 8388608 | tf_op jit(solution)/shard_map/earlier_blocks/pallas_call | solution.py:573
  (1 shorter events, 0.0 us)
Async XLA Ops:
  0.0 6.3 %copy-start = (bf16[256,1024]{1,0:T(8,128)(2,1)S(1)}, bf16[256,1024]{1,0:T(8,128)(2,1)}, u32[]{:S(2)}) copy-start(bf16[256,1024]{1,0:T(8,128)(2,1)} %refs_0_.3) | copy-start | bytes 1572868
  3.2 11.2 %collective-permute-start = (bf16[128,640]{1,0:T(8,128)(2,1)S(1)}, bf16[128,640]{1,0:T(8,128)(2,1)S(1)}, u32[]{:S(2)}, u32[]{:S(2)}) collective-permute-start(bf16[128,640]{1,0:T(8,128)(2,1)S(1)} %get-tuple-element.46), channel_id=1, source_target_pairs={{0,2},{1,3},{2,4},{3,5},{4,6},{5,7},{6,8},{7,9},{8,10},{9,11},{10,... | collective-permute-start | bytes 491528 | tf_op jit(solution)/shard_map/ppermute | solution.py:461
  7.6 6.8 %collective-permute-start.1 = (bf16[128,640]{1,0:T(8,128)(2,1)S(1)}, bf16[128,640]{1,0:T(8,128)(2,1)S(1)}, u32[]{:S(2)}, u32[]{:S(2)}) collective-permute-start(bf16[128,640]{1,0:T(8,128)(2,1)S(1)} %get-tuple-element.46), channel_id=1, source_target_pairs={{0,1},{1,0},{2,3},{3,2},{4,5},{5,4},{6,7},{7,6},{8,9},{9,8},{10,11... | collective-permute-start | bytes 491528 | tf_op jit(solution)/shard_map/ppermute | solution.py:461
  7.7 8.4 %collective-permute-start.3 = (bf16[128,640]{1,0:T(8,128)(2,1)S(1)}, bf16[128,640]{1,0:T(8,128)(2,1)S(1)}, u32[]{:S(2)}, u32[]{:S(2)}) collective-permute-start(bf16[128,640]{1,0:T(8,128)(2,1)S(1)} %get-tuple-element.46), channel_id=1, source_target_pairs={{0,1},{1,4},{2,3},{3,6},{4,5},{5,8},{6,7},{7,10},{8,9},{9,12},{10,... | collective-permute-start | bytes 491528 | tf_op jit(solution)/shard_map/ppermute | solution.py:461
  14.5 1.5 %collective-permute-start.2 = (bf16[128,640]{1,0:T(8,128)(2,1)S(1)}, bf16[128,640]{1,0:T(8,128)(2,1)S(1)}, u32[]{:S(2)}, u32[]{:S(2)}) collective-permute-start(bf16[128,640]{1,0:T(8,128)(2,1)S(1)} %collective-permute-done.refs_0_), channel_id=1, source_target_pairs={{0,1},{1,0},{2,3},{3,2},{4,5},{5,4},{6,7},{7,6},{8,9},{9,8},{10,11... | collective-permute-start | bytes 491528 | tf_op jit(solution)/shard_map/ppermute | solution.py:461

commit v6 on v5

--- a/solution.py
+++ b/solution.py
@@ -33,25 +33,31 @@
     return dot(left_high, right_high) + (dot(left_high, right_low) + dot(left_low, right_high))
 
 
+def dot_joined(left, right):
+    (left_high, left_low), (right_high, right_low) = left, right
+    return dot(
+        jnp.concatenate([left_high, left_low, left_high], axis=1),
+        jnp.concatenate([right_high, right_high, right_low], axis=0),
+    )
+
+
 def unit_inverses(strict_parts):
     length = strict_parts[0].shape[0]
     rows = lax.broadcasted_iota(jnp.int32, (length, length), 0)
     columns = lax.broadcasted_iota(jnp.int32, (length, length), 1)
     identity = (rows == columns).astype(F32)
     results = [identity - part for part in strict_parts]
-    powers = [halves(part) for part in strict_parts]
-    powers = [dot_halves(power, power) for power in powers]
-    reach = 4
+    powers = list(strict_parts)
+    reach = 2
     while reach < length:
         for index, (result, power) in enumerate(zip(results, powers)):
-            high, low = halves(jnp.concatenate([power, result], axis=0))
-            weights = (high[:length], low[:length])
-            product = dot_halves((high, low), weights)
-            powers[index] = product[:length]
-            results[index] = result + product[length:]
+            power = halves(power)
+            powers[index] = dot_joined(power, power)
+            if reach > 2:
+                results[index] = result + dot_joined(halves(result), power)
         reach = reach * 2
     return [
-        result + dot_halves(halves(result), halves(power))
+        result + dot_joined(halves(result), halves(power))
         for result, power in zip(results, powers)
     ]
 
@@ -113,13 +119,13 @@
         jnp.concatenate([facing[half:, :half], reflect_float[half:], facing[half:, half:]], axis=1)
     )
     first, second = unit_inverses([chained[:half, :half], chained[half:, half:]])
-    upper = dot_halves(halves(first), wide)
-    reach = halves(dot_halves(scaled_second, halves(second)))
-    bridge = dot_halves(reach, across)
+    upper = dot_joined(halves(first), wide)
+    reach = halves(dot_joined(scaled_second, halves(second)))
+    bridge = dot_joined(reach, across)
     upper_halves = halves(upper)
-    own = dot_halves(scaled_first, upper_halves)
-    later = dot_halves(reach, tall)
-    change = (own + later[:, :wide_size - half]) - dot_halves(halves(bridge), upper_halves)
+    own = dot_joined(scaled_first, upper_halves)
+    later = dot_joined(reach, tall)
+    change = (own + later[:, :wide_size - half]) - dot_joined(halves(bridge), upper_halves)
     partial_ref[:, :half] = second
     partial_ref[:, half:length] = chained[half:, :half]
     partial_ref[:, length : 2 * length] = facing[half:, :]
@@ -416,8 +422,10 @@
 
     if slots == 1:
 
-        @pl.when(present > odd.astype(jnp.int32))
-        def _():
+        work = (present > odd.astype(jnp.int32)).astype(jnp.int32)
+
+        @pl.loop(0, work)
+        def _(_):
             lax.cond(
                 odd,
                 lambda: choose(2, longest - 1, True),
@@ -543,7 +551,7 @@
     )
     turned = state[0]
     *apart, present = lax.optimization_barrier((*apart, present))
-    early_heads = head_count
+    early_heads = max(1, 5 * head_count // 8)
     if slots == 1:
         done = pl.pallas_call(
             functools.partial(early_kernel, range(early_heads)),

time: 16.9 us -> 16.4 us (0.970)
  the two profiles are of different devices: /device:TPU:0 before, /device:TPU:1 now
where the time goes in v6:
time: 16.4 us; the launch traced here: 16.3 us
  Pallas kernels  9.7 us (59%)
  starting transfers between devices  4.81 us (29%)
  waiting for transfers between devices  1.56 us (10%)
  between operations  0.21 us (1%)
    ppermute x4, starting transfers between devices, permuted(): lax.ppermute(value, AXES, [(i, target(i) % count) for i in range(count)])  4.81 us
    pallas_call x1, Pallas kernels, local(): pl.pallas_call(key_kernel, out_shape=(shape((head_size, wide_size + lengt...  3.03 us
    pallas_call x1, Pallas kernels, local(): pl.pallas_call(functools.partial(other_queries, range(first, head_count),...  2.77 us
    ppermute x4, waiting for transfers between devices, permuted(): lax.ppermute(value, AXES, [(i, target(i) % count) for i in range(count)])  1.56 us
    pallas_call x1, Pallas kernels, local(): pl.pallas_call(functools.partial(nearest_kernel, head_count, early_heads)...  1.37 us
    pallas_call x1, Pallas kernels, local(): pl.pallas_call(functools.partial(first_queries, range(first)), out_shape=...  1.36 us
    pallas_call x1, Pallas kernels, local(): pl.pallas_call(functools.partial(early_kernel, range(early_heads)), out_s...  0.86 us
  transfers between devices with their start and end apart: 4, of which 1 were waited for; matrix products, arithmetic and copies ran while one was open for 0% of the time, Pallas kernels for 39%

profile of v6, /device:TPU:1, one launch (start us, length us, event | category | flops | bytes accessed | tf_op | source)
XLA Modules:
  0.0 16.3 jit_solution(5253112610701477280)
XLA Ops:
  0.0 0.0 copy-start
  0.0 3.0 %key_side.1 = (bf16[128,640]{1,0:T(8,128)(2,1)S(1)}, f32[128,768]{1,0:T(8,128)S(1)}, f32[8,256]{1,0:T(8,128)S(1)}, bf16[128,512]{1,0:T(8,128)(2,1)S(1)}, bf16[25...) custom-call(bf16[256,128]{1,0:T(8,128)(2,1)} %reflect_hbm.1, bf16[256,128]{1,0:T(8,128)(2,1)} %keys_hbm.1, ...), custom_call_target="tpu_custom_call" | custom-call | flops 671088640 | bytes 524288 | tf_op jit(solution)/shard_map/key_side/pallas_call | solution.py:480
  3.0 2.1 %collective-permute-start = (bf16[128,640]{1,0:T(8,128)(2,1)S(1)}, bf16[128,640]{1,0:T(8,128)(2,1)S(1)}, u32[]{:S(2)}, u32[]{:S(2)}) collective-permute-start(bf16[128,640]{1,0:T(8,128)(2,1)S(1)} %get-tuple-element.46), channel_id=1, source_target_pairs={{0,2},{1,3},{2,4},{3,5},{4,6},{5,7},{6,8},{7,9},{8,10},{9,11},{10,... | collective-permute-start | bytes 491528 | tf_op jit(solution)/shard_map/ppermute | solution.py:469
  5.2 0.0 copy-done
  5.2 1.4 %first_queries.1 = (bf16[256,256]{1,0:T(8,128)(2,1)S(1)}, f32[256,256]{1,0:T(8,128)S(1)}, f32[256,256]{1,0:T(8,128)S(1)}, f32[256,256]{1,0:T(8,128)S(1)}, bf16[256,768]{1,0:T(8,128)(2,1)S(1)}) custom-call(bf16[256,1024]{1,0:T(8,128)(2,1)S(1)} %copy-done, bf16[128,512]{1,0:T(8,128)(2,1)S(1)} %get-tuple-element.32.refs_1_, ...), custom_call_target="tpu_custom_call" | custom-call | flops 335544320 | bytes 2097152 | tf_op jit(solution)/shard_map/first_queries/pallas_call | solution.py:516
  6.5 1.0 %collective-permute-start.1 = (bf16[128,640]{1,0:T(8,128)(2,1)S(1)}, bf16[128,640]{1,0:T(8,128)(2,1)S(1)}, u32[]{:S(2)}, u32[]{:S(2)}) collective-permute-start(bf16[128,640]{1,0:T(8,128)(2,1)S(1)} %get-tuple-element.46), channel_id=1, source_target_pairs={{0,1},{1,0},{2,3},{3,2},{4,5},{5,4},{6,7},{7,6},{8,9},{9,8},{10,11... | collective-permute-start | bytes 491528 | tf_op jit(solution)/shard_map/ppermute | solution.py:469
  7.5 1.2 %collective-permute-start.3 = (bf16[128,640]{1,0:T(8,128)(2,1)S(1)}, bf16[128,640]{1,0:T(8,128)(2,1)S(1)}, u32[]{:S(2)}, u32[]{:S(2)}) collective-permute-start(bf16[128,640]{1,0:T(8,128)(2,1)S(1)} %get-tuple-element.46), channel_id=1, source_target_pairs={{0,1},{1,4},{2,3},{3,6},{4,5},{5,8},{6,7},{7,10},{8,9},{9,12},{10,... | collective-permute-start | bytes 491528 | tf_op jit(solution)/shard_map/ppermute | solution.py:469
  8.7 2.8 %other_queries.1 = (bf16[256,1024]{1,0:T(8,128)(2,1)S(1)}, f32[256,1024]{1,0:T(8,128)S(1)}, f32[256,1024]{1,0:T(8,128)S(1)}, f32[256,1024]{1,0:T(8,128)S(1)}, s32[8,128]{1,0:T(8,128)S(1)}) custom-call(s32[32]{0:T(128)} %docs_hbm.1, bf16[256,1024]{1,0:T(8,128)(2,1)S(1)} %copy-done, bf16[128,512]{1,0:T(8,128)(2,1)S(1)} %get-tuple-element.32.refs_1_, ...), custom_call_target="tpu_custom_call" | custom-call | flops 1006632960 | bytes 6291456 | tf_op jit(solution)/shard_map/other_queries/pallas_call | solution.py:530
  11.5 1.6 %collective-permute-done.refs_0_ = bf16[128,640]{1,0:T(8,128)(2,1)S(1)} collective-permute-done((bf16[128,640]{1,0:T(8,128)(2,1)S(1)}, bf16[128,640]{1,0:T(8,128)(2,1)S(1)}, u32[]{:S(2)}, u32[]{:S(2)}) %collective-permute-start) | collective-permute-done | bytes 163872 | tf_op jit(solution)/shard_map/ppermute | solution.py:469
  13.0 0.0 collective-permute-done.1.beside_ref.refs_3_
  13.0 0.9 %early_heads.1.done_ref = bf16[256,640]{1,0:T(8,128)(2,1)S(1)} custom-call(s32[8,128]{1,0:T(8,128)S(1)} %get-tuple-element.44.present_ref, bf16[128,640]{1,0:T(8,128)(2,1)S(1)} %collective-permute-done.1.beside_ref.refs_3_, bf16[256,1024]{1,0:T(8,128)(2,1)S(1)} %get-tuple-element.47.refs_0_.refs_4_, f32[256,1024]{1,0:T(8,128)S(1)} %get-tuple-element.48.refs_1_, ...), custom_call_target="tpu_custom_call" | custom-call | tf_op jit(solution)/shard_map/early_heads/pallas_call | solution.py:556
  13.9 0.5 %collective-permute-start.2 = (bf16[128,640]{1,0:T(8,128)(2,1)S(1)}, bf16[128,640]{1,0:T(8,128)(2,1)S(1)}, u32[]{:S(2)}, u32[]{:S(2)}) collective-permute-start(bf16[128,640]{1,0:T(8,128)(2,1)S(1)} %collective-permute-done.refs_0_), channel_id=1, source_target_pairs={{0,1},{1,0},{2,3},{3,2},{4,5},{5,4},{6,7},{7,6},{8,9},{9,8},{10,11... | collective-permute-start | bytes 491528 | tf_op jit(solution)/shard_map/ppermute | solution.py:469
  14.4 1.4 %nearest_block.1 = (f32[256,1024]{1,0:T(8,128)S(1)}, f32[256,1024]{1,0:T(8,128)S(1)}, f32[256,1024]{1,0:T(8,128)S(1)}, bf16[256,1024]{1,0:T(8,128)(2,1)}) custom-call(s32[8,128]{1,0:T(8,128)S(1)} %get-tuple-element.44.present_ref, bf16[128,640]{1,0:T(8,128)(2,1)S(1)} %collective-permute-done.1.beside_ref.refs_3_, bf16[256,640]{1,0:T(8,128)(2,1)S(1)} %early_heads.1.done_ref, ...), custom_call_target="tpu_custom_call" | custom-call | flops 268435456 | bytes 2097152 | tf_op jit(solution)/shard_map/nearest_block/pallas_call | solution.py:570
  15.8 0.0 collective-permute-done.3.refs_2_
  15.8 0.0 collective-permute-done.2.refs_1_
  15.8 0.3 %earlier_blocks.1 = bf16[256,1024]{1,0:T(8,128)(2,1)} custom-call(s32[8,128]{1,0:T(8,128)S(1)} %get-tuple-element.44.present_ref, bf16[128,640]{1,0:T(8,128)(2,1)S(1)} %collective-permute-done.refs_0_, bf16[128,640]{1,0:T(8,128)(2,1)S(1)} %collective-permute-done.2.refs_1_, ...), custom_call_target="tpu_custom_call", output_to_operand_aliasing={{}: (9, {})} | custom-call | flops 805306368 | bytes 8388608 | tf_op jit(solution)/shard_map/earlier_blocks/pallas_call | solution.py:581
Async XLA Ops:
  0.0 5.2 %copy-start = (bf16[256,1024]{1,0:T(8,128)(2,1)S(1)}, bf16[256,1024]{1,0:T(8,128)(2,1)}, u32[]{:S(2)}) copy-start(bf16[256,1024]{1,0:T(8,128)(2,1)} %refs_0_.3) | copy-start | bytes 1572868
  3.0 10.0 %collective-permute-start = (bf16[128,640]{1,0:T(8,128)(2,1)S(1)}, bf16[128,640]{1,0:T(8,128)(2,1)S(1)}, u32[]{:S(2)}, u32[]{:S(2)}) collective-permute-start(bf16[128,640]{1,0:T(8,128)(2,1)S(1)} %get-tuple-element.46), channel_id=1, source_target_pairs={{0,2},{1,3},{2,4},{3,5},{4,6},{5,7},{6,8},{7,9},{8,10},{9,11},{10,... | collective-permute-start | bytes 491528 | tf_op jit(solution)/shard_map/ppermute | solution.py:469
  6.5 6.5 %collective-permute-start.1 = (bf16[128,640]{1,0:T(8,128)(2,1)S(1)}, bf16[128,640]{1,0:T(8,128)(2,1)S(1)}, u32[]{:S(2)}, u32[]{:S(2)}) collective-permute-start(bf16[128,640]{1,0:T(8,128)(2,1)S(1)} %get-tuple-element.46), channel_id=1, source_target_pairs={{0,1},{1,0},{2,3},{3,2},{4,5},{5,4},{6,7},{7,6},{8,9},{9,8},{10,11... | collective-permute-start | bytes 491528 | tf_op jit(solution)/shard_map/ppermute | solution.py:469
  7.5 8.3 %collective-permute-start.3 = (bf16[128,640]{1,0:T(8,128)(2,1)S(1)}, bf16[128,640]{1,0:T(8,128)(2,1)S(1)}, u32[]{:S(2)}, u32[]{:S(2)}) collective-permute-start(bf16[128,640]{1,0:T(8,128)(2,1)S(1)} %get-tuple-element.46), channel_id=1, source_target_pairs={{0,1},{1,4},{2,3},{3,6},{4,5},{5,8},{6,7},{7,10},{8,9},{9,12},{10,... | collective-permute-start | bytes 491528 | tf_op jit(solution)/shard_map/ppermute | solution.py:469
  13.9 1.9 %collective-permute-start.2 = (bf16[128,640]{1,0:T(8,128)(2,1)S(1)}, bf16[128,640]{1,0:T(8,128)(2,1)S(1)}, u32[]{:S(2)}, u32[]{:S(2)}) collective-permute-start(bf16[128,640]{1,0:T(8,128)(2,1)S(1)} %collective-permute-done.refs_0_), channel_id=1, source_target_pairs={{0,1},{1,0},{2,3},{3,2},{4,5},{5,4},{6,7},{7,6},{8,9},{9,8},{10,11... | collective-permute-start | bytes 491528 | tf_op jit(solution)/shard_map/ppermute | solution.py:469
